TPU v7x, 32 devices: a whole 2x2x4 slice. The times are simulated.
32 devices in a mesh: dp: 2 (over x), row: 4 (over y, core), col: 4 (over z).
Axes of the slice: x: 2, y: 2, z: 4, core: 2. Of those that a mesh axis runs over, the one named last changes fastest.
Arguments:
- frames: bfloat16 [4, 1500, 768], P('dp', 'col'), may hold values from -34 to 34
- ln1_gain: float32 [768], P('row'), may hold values from 0.25 to 1.75
- ln1_bias: float32 [768], P('row'), may hold values from -1 to 1
- w_query: bfloat16 [768, 768], P('row', 'col'), may hold values from -0.21875 to 0.21875
- b_query: float32 [768], replicated, may hold values from -1.5 to 1.5
- w_key: bfloat16 [768, 768], P('row', 'col'), may hold values from -0.21875 to 0.21875
- w_value: bfloat16 [768, 768], P('row', 'col'), may hold values from -0.21875 to 0.21875
- b_value: float32 [768], replicated, may hold values from -0.25 to 0.25
- w_out: bfloat16 [768, 768], P('col', 'row'), may hold values from -2 to 2
- b_out: float32 [768], P('row'), may hold values from -1.5 to 1.5
- ln2_gain: float32 [768], P('row'), may hold values from 0.25 to 1.75
- ln2_bias: float32 [768], P('row'), may hold values from -1 to 1
- w_fc1: bfloat16 [768, 3072], P('row', 'col'), may hold values from -0.21875 to 0.21875
- b_fc1: float32 [3072], replicated, may hold values from -1.5 to 1.5
- w_fc2: bfloat16 [768, 3072], P('row', 'col'), may hold values from -0.109375 to 0.109375
- b_fc2: float32 [768], P('row'), may hold values from -1.5 to 1.5
- cotangent: bfloat16 [4, 1500, 768], P('dp', 'col'), may hold values from -6 to 6
Outputs:
- block_out: bfloat16 [4, 1500, 768], P('dp', 'col')
- grad_frames: bfloat16 [4, 1500, 768], P('dp', 'col')
- grad_ln1_gain: float32 [768], P('row')
- grad_ln1_bias: float32 [768], P('row')
- grad_w_query: float32 [768, 768], P('row', 'col')
- grad_b_query: float32 [768], P('col')
- grad_w_key: float32 [768, 768], P('row', 'col')
- grad_w_value: float32 [768, 768], P('row', 'col')
- grad_b_value: float32 [768], P('col')
- grad_w_out: float32 [768, 768], P('col', 'row')
- grad_b_out: float32 [768], P('row')
- grad_ln2_gain: float32 [768], P('row')
- grad_ln2_bias: float32 [768], P('row')
- grad_w_fc1: float32 [768, 3072], P('row', 'col')
- grad_b_fc1: float32 [3072], P('col')
- grad_w_fc2: float32 [768, 3072], P('row', 'col')
- grad_b_fc2: float32 [768], P('row')
All inputs are finite; a program needn't handle non-finite values.
Results may differ from a plain program's by a relative error of at most 0.025.
Values may be sent and summed in bfloat16 or wider, within the bound.
A program may use at most 128 MiB of HBM per device.

v0:
```python
import jax
import jax.numpy as jnp
from jax import lax
from jax.sharding import PartitionSpec as P

HEAD = 64
D = 768


def gather_cols(tensor):
    return lax.all_gather(tensor, "col", axis=1, tiled=True)


def reduce_cols(tensor):
    return lax.psum_scatter(
        tensor.astype(jnp.bfloat16), "col", scatter_dimension=1, tiled=True
    ).astype(jnp.float32)


def gather_features(tensor):
    return lax.all_gather(tensor, "row", axis=2, tiled=True)


def sum_features(tensor):
    return lax.psum_scatter(
        tensor.astype(jnp.bfloat16), "row", scatter_dimension=2, tiled=True
    ).astype(jnp.float32)


def feature_totals(first_part, second_part):
    return lax.psum((first_part, second_part), "row")


def forward_mix(operand, weight):
    return jnp.einsum("cti,io->cto", operand, weight, preferred_element_type=jnp.float32)


def turned_mix(operand, weight):
    return jnp.einsum("cti,oi->cto", operand, weight, preferred_element_type=jnp.float32)


def backward_mix(gradient, weight):
    return jnp.einsum("cto,io->cti", gradient, weight, preferred_element_type=jnp.float32)


def turned_back(gradient, weight):
    return jnp.einsum("cto,oi->cti", gradient, weight, preferred_element_type=jnp.float32)


def weight_grad(operand, gradient):
    return jnp.einsum("cti,cto->io", operand, gradient, preferred_element_type=jnp.float32)


def turned_grad(gradient, operand):
    return jnp.einsum("cto,cti->oi", gradient, operand, preferred_element_type=jnp.float32)


def column_sums(gradient):
    return jnp.sum(gradient, axis=(0, 1), dtype=jnp.float32)


def place_piece(vector, piece_index, piece_count):
    piece_size = vector.shape[0]
    filled = jnp.zeros((piece_size * piece_count,), jnp.float32)
    return lax.dynamic_update_slice(filled, vector, (piece_index * piece_size,))


def take_piece(vector, piece_index, piece_size):
    return lax.dynamic_slice_in_dim(vector, piece_index * piece_size, piece_size)


def gelu_exact(tensor):
    return jax.nn.gelu(tensor, approximate=False)


def norm_forward(tensor, norm_gain, norm_bias):
    totals = jnp.sum(tensor, axis=-1)
    squares = jnp.sum(tensor * tensor, axis=-1)
    totals, squares = feature_totals(totals, squares)
    average = totals / D
    variance = squares / D - average * average
    inv_std = lax.rsqrt(variance + 1e-05)
    scaled = (tensor - average[..., None]) * inv_std[..., None]
    return ((scaled * norm_gain + norm_bias).astype(jnp.bfloat16), scaled, inv_std)


def norm_backward(gradient, scaled, inv_std, norm_gain):
    weighted = gradient * norm_gain
    first_sum = jnp.sum(weighted, axis=-1)
    second_sum = jnp.sum(weighted * scaled, axis=-1)
    first_sum, second_sum = feature_totals(first_sum, second_sum)
    grad_in = inv_std[..., None] * (
        weighted - first_sum[..., None] / D - scaled * second_sum[..., None] / D
    )
    return (grad_in, jnp.sum(gradient * scaled, axis=(0, 1)), jnp.sum(gradient, axis=(0, 1)))


def split_heads(tensor):
    head_total = tensor.shape[-1] // HEAD
    return tensor.reshape(tensor.shape[0], head_total, HEAD)


def attend_clip(inputs):
    query_part, key_whole, value_whole = inputs
    query_heads = split_heads(query_part)
    key_heads = split_heads(key_whole)
    value_heads = split_heads(value_whole)
    scores = (
        jnp.einsum("qhd,khd->hqk", query_heads, key_heads, preferred_element_type=jnp.float32)
        * 0.125
    )
    highest = jnp.max(scores, axis=-1, keepdims=True)
    log_total = highest + jnp.log(jnp.sum(jnp.exp(scores - highest), axis=-1, keepdims=True))
    probability = jnp.exp(scores - log_total).astype(jnp.bfloat16)
    attended = jnp.einsum(
        "hqk,khd->qhd", probability, value_heads, preferred_element_type=jnp.float32
    )
    return (attended.reshape(query_part.shape).astype(jnp.bfloat16), log_total[..., 0])


def attend_back(inputs):
    query_part, key_whole, value_whole, log_total, grad_attended = inputs
    query_heads = split_heads(query_part)
    key_heads = split_heads(key_whole)
    value_heads = split_heads(value_whole)
    grad_heads = split_heads(grad_attended)
    scores = (
        jnp.einsum("qhd,khd->hqk", query_heads, key_heads, preferred_element_type=jnp.float32)
        * 0.125
    )
    probability = jnp.exp(scores - log_total[..., None])
    grad_prob = jnp.einsum(
        "qhd,khd->hqk", grad_heads, value_heads, preferred_element_type=jnp.float32
    )
    row_dot = jnp.sum(probability * grad_prob, axis=-1, keepdims=True)
    grad_scores = (probability * (grad_prob - row_dot)).astype(jnp.bfloat16)
    grad_query = (
        jnp.einsum("hqk,khd->qhd", grad_scores, key_heads, preferred_element_type=jnp.float32)
        * 0.125
    )
    grad_keys = (
        jnp.einsum("hqk,qhd->khd", grad_scores, query_heads, preferred_element_type=jnp.float32)
        * 0.125
    )
    grad_values = jnp.einsum(
        "hqk,qhd->khd",
        probability.astype(jnp.bfloat16),
        grad_heads,
        preferred_element_type=jnp.float32,
    )
    return (
        grad_query.reshape(query_part.shape).astype(jnp.bfloat16),
        grad_keys.reshape(key_whole.shape),
        grad_values.reshape(value_whole.shape),
    )


def local(
    frames,
    ln1_gain,
    ln1_bias,
    w_query,
    b_query,
    w_key,
    w_value,
    b_value,
    w_out,
    b_out,
    ln2_gain,
    ln2_bias,
    w_fc1,
    b_fc1,
    w_fc2,
    b_fc2,
    cotangent,
):
    row_count = lax.axis_size("row")
    row_at = lax.axis_index("row")
    col_at = lax.axis_index("col")
    head_width = w_query.shape[1]
    hidden_part = w_fc1.shape[1]
    feature_part = frames.shape[2] // row_count
    clip_count = frames.shape[0]
    frame_count = frames.shape[1]
    inputs_wide = lax.dynamic_slice_in_dim(frames, row_at * feature_part, feature_part, 2).astype(
        jnp.float32
    )
    cotangent_part = lax.dynamic_slice_in_dim(cotangent, row_at * feature_part, feature_part, 2)
    bias_query = take_piece(b_query, row_at, head_width)
    bias_value = take_piece(b_value, row_at, head_width)
    bias_hidden = take_piece(b_fc1, row_at, hidden_part)
    offsets = jnp.concatenate([bias_query, jnp.zeros_like(bias_query), bias_value])
    packed = jnp.concatenate([w_query, w_key, w_value, w_out.T, w_fc1, w_fc2], axis=1)
    weights = lax.all_to_all(gather_cols(packed), "row", split_axis=1, concat_axis=0, tiled=True)
    joint_end = 3 * head_width
    out_end = 4 * head_width
    hidden_end = out_end + hidden_part
    w_joint = weights[:, :joint_end]
    out_rows = weights[:, joint_end:out_end]
    first_ff = weights[:, out_end:hidden_end]
    second_ff = weights[:, hidden_end:]
    normed, scaled_one, inv_std_one = norm_forward(inputs_wide, ln1_gain, ln1_bias)
    normed_all = gather_features(normed)
    projected = (forward_mix(normed_all, w_joint) + offsets).astype(jnp.bfloat16)
    pair_whole = gather_cols(projected[..., head_width:])
    query_part = projected[..., :head_width]
    key_whole = pair_whole[..., :head_width]
    value_whole = pair_whole[..., head_width:]
    attended, log_total = lax.map(attend_clip, (query_part, key_whole, value_whole))
    branch = sum_features(turned_mix(attended, out_rows))
    residual = inputs_wide + branch + b_out
    normed_two, scaled_two, inv_std_two = norm_forward(residual, ln2_gain, ln2_bias)
    normed_two_all = gather_features(normed_two)
    pre_act = forward_mix(normed_two_all, first_ff) + bias_hidden
    activated, gelu_pull = jax.vjp(gelu_exact, pre_act)
    hidden = activated.astype(jnp.bfloat16)
    block_out = (residual + sum_features(turned_mix(hidden, second_ff)) + b_fc2).astype(
        jnp.bfloat16
    )
    cotangent_all = gather_features(cotangent_part)
    grad_second = turned_grad(cotangent_all, hidden)
    hidden_terms = turned_back(cotangent_all, second_ff)
    d_pre = gelu_pull(hidden_terms)[0].astype(jnp.bfloat16)
    grad_first = weight_grad(normed_two_all, d_pre)
    normed_two_terms = backward_mix(d_pre, first_ff)
    d_normed_two = sum_features(normed_two_terms)
    d_residual_norm, gain_two_part, bias_two_part = norm_backward(
        d_normed_two, scaled_two, inv_std_two, ln2_gain
    )
    d_residual = cotangent_part.astype(jnp.float32) + d_residual_norm
    d_branch = d_residual.astype(jnp.bfloat16)
    d_branch_all = gather_features(d_branch)
    grad_out_rows = turned_grad(d_branch_all, attended)
    attended_terms = turned_back(d_branch_all, out_rows)
    d_attended = attended_terms.astype(jnp.bfloat16)
    d_query, key_grad_part, value_grad_part = lax.map(
        attend_back, (query_part, key_whole, value_whole, log_total, d_attended)
    )
    pair_terms = jnp.concatenate([key_grad_part, value_grad_part], axis=-1)
    pair_grads = reduce_cols(pair_terms)
    d_joint = jnp.concatenate([d_query, pair_grads.astype(jnp.bfloat16)], axis=-1)
    grad_joint = weight_grad(normed_all, d_joint)
    joint_terms = backward_mix(d_joint, w_joint)
    d_normed = sum_features(joint_terms)
    d_frames_norm, gain_one_part, bias_one_part = norm_backward(
        d_normed, scaled_one, inv_std_one, ln1_gain
    )
    grad_frames = (d_residual + d_frames_norm).astype(jnp.bfloat16)
    grad_pack = jnp.concatenate([grad_joint, grad_out_rows, grad_first, grad_second], axis=1)
    grad_pack = reduce_cols(
        lax.all_to_all(
            grad_pack.astype(jnp.bfloat16), "row", split_axis=0, concat_axis=1, tiled=True
        ).astype(grad_pack.dtype)
    )
    grad_pack = lax.psum(grad_pack.astype(jnp.bfloat16), "dp").astype(jnp.float32)
    joint_sums = column_sums(d_joint)
    (
        gain_one,
        bias_one,
        gain_two,
        bias_two,
        query_total,
        value_total,
        out_total,
        hidden_total,
        last_total,
    ) = lax.psum(
        (
            place_piece(gain_one_part, row_at, row_count),
            place_piece(bias_one_part, row_at, row_count),
            place_piece(gain_two_part, row_at, row_count),
            place_piece(bias_two_part, row_at, row_count),
            place_piece(joint_sums[:head_width], row_at, row_count),
            place_piece(joint_sums[2 * head_width :], row_at, row_count),
            place_piece(column_sums(d_branch), row_at, row_count),
            place_piece(column_sums(d_pre), row_at, row_count),
            place_piece(column_sums(cotangent_part), row_at, row_count),
        ),
        ("dp", "row", "col"),
    )
    outputs_whole = gather_features(jnp.concatenate([block_out, grad_frames], axis=-1))
    outputs_whole = outputs_whole.reshape(clip_count, frame_count, row_count, 2, feature_part)
    block_whole = outputs_whole[:, :, :, 0, :].reshape(
        clip_count, frame_count, row_count * feature_part
    )
    grad_whole = outputs_whole[:, :, :, 1, :].reshape(
        clip_count, frame_count, row_count * feature_part
    )
    return (
        block_whole,
        grad_whole,
        take_piece(gain_one, row_at, feature_part),
        take_piece(bias_one, row_at, feature_part),
        grad_pack[:, :head_width],
        take_piece(query_total, col_at, head_width),
        grad_pack[:, head_width : 2 * head_width],
        grad_pack[:, 2 * head_width : joint_end],
        take_piece(value_total, col_at, head_width),
        grad_pack[:, joint_end:out_end].T,
        take_piece(out_total, row_at, feature_part),
        take_piece(gain_two, row_at, feature_part),
        take_piece(bias_two, row_at, feature_part),
        grad_pack[:, out_end:hidden_end],
        take_piece(hidden_total, col_at, hidden_part),
        grad_pack[:, hidden_end:],
        take_piece(last_total, row_at, feature_part),
    )


def solution(mesh):
    placed = (
        P("dp", "col", None),
        P("row"),
        P("row"),
        P("row", "col"),
        P(),
        P("row", "col"),
        P("row", "col"),
        P(),
        P("col", "row"),
        P("row"),
        P("row"),
        P("row"),
        P("row", "col"),
        P(),
        P("row", "col"),
        P("row"),
        P("dp", "col", None),
    )
    return jax.shard_map(
        local,
        mesh=mesh,
        in_specs=placed,
        out_specs=(
            P("dp", "col", None),
            P("dp", "col", None),
            P("row"),
            P("row"),
            P("row", "col"),
            P("col"),
            P("row", "col"),
            P("row", "col"),
            P("col"),
            P("col", "row"),
            P("row"),
            P("row"),
            P("row"),
            P("row", "col"),
            P("col"),
            P("row", "col"),
            P("row"),
        ),
        check_vma=False,
    )
```

profile of v0, /device:TPU:0, one launch (start us, length us, event | category | flops | bytes accessed | tf_op | source)
XLA Modules:
  0.0 722.0 jit_solution(2136149255657252971)
XLA Ops:
  9.2 2.2 concatenate.29
  11.4 72.8 %all-gather.10.cloned.1.call-done = bf16[192,9216]{1,0:T(8,128)(2,1)} async-done(((bf16[192,2304]{1,0:T(8,128)(2,1)}), bf16[192,9216]{1,0:T(8,128)(2,1)}) %all-gather.10.cloned.1.call-update) | async-done | bytes 3538960 | tf_op jit(solution)/shard_map/all_gather | solution.py:11
  84.2 4.0 copy.128
  88.2 4.9 all-to-all-start
  94.7 41.2 %all-reduce.5 = (f32[2,375]{1,0:T(2,128)S(1)}, f32[2,375]{1,0:T(2,128)S(1)}) all-reduce(f32[2,375]{1,0:T(2,128)S(1)} %get-tuple-element.232, f32[2,375]{1,0:T(2,128)S(1)} %get-tuple-element.231), channel_id=1, replica_groups=mesh['dp'=2,'row'=4,'col'=4] {'row'}, use_global_device_ids=true, to_apply=%region_3.0 | all-reduce | flops 1500 | bytes 12000 | tf_op jit(solution)/shard_map/psum | solution.py:31
  139.1 14.6 %all-gather.8.cloned.1.call-done = bf16[2,375,768]{1,2,0:T(8,128)(2,1)} async-done(((bf16[2,375,192]{1,2,0:T(8,128)(2,1)}), bf16[2,375,768]{1,2,0:T(8,128)(2,1)}) %all-gather.8.cloned.1.call-update) | async-done | bytes 1152016 | tf_op jit(solution)/shard_map/all_gather | solution.py:21
  153.6 2.5 add_convert_fusion.1
  156.2 1.8 copy.101
  158.1 49.6 %all-gather.12.cloned.1.call-done = bf16[2,1500,384]{2,0,1:T(2,128)(2,1)} async-done(((bf16[2,375,384]{2,0,1:T(2,128)(2,1)}), bf16[2,1500,384]{2,0,1:T(2,128)(2,1)}) %all-gather.12.cloned.1.call-update) | async-done | bytes 2304016 | tf_op jit(solution)/shard_map/all_gather | solution.py:11
  207.7 5.6 fusion.47
  213.3 3.5 copy.102
  216.9 3.6 copy.103
  220.5 8.1 %while.26 = (s32[]{:T(128)}, bf16[2,375,192]{1,2,0:T(8,128)(2,1)S(1)}, f32[2,3,375]{2,1,0:T(4,128)S(1)}, bf16[2,1500,192]{1,2,0:T(8,128)(2,1)S(1)}, bf16[2,375,1...) while((s32[]{:T(128)}, bf16[2,375,192]{1,2,0:T(8,128)(2,1)S(1)}, ...), condition=%wide.region_7.8_spmd, body=%wide.region_4.7_spmd.sunk | while | flops 445570880 | bytes 24619588 | solution.py:209
  221.8 1.3 exponential_reduce_fusion.2
  223.2 1.4 fusion.97
  225.9 1.3 exponential_reduce_fusion.2
  227.2 1.4 fusion.97
  228.7 2.7 convolution_convert_fusion.2
  231.5 24.5 %reduce-scatter.6.cloned.1.call-done = bf16[2,375,192]{1,2,0:T(8,128)(2,1)} async-done(((bf16[2,375,768]{1,2,0:T(8,128)(2,1)}), bf16[2,375,192]{1,2,0:T(8,128)(2,1)}) %reduce-scatter.6.cloned.1.call-update) | async-done | bytes 288016 | tf_op jit(solution)/shard_map/reduce_scatter | solution.py:25
  257.2 5.8 all-reduce.4
  263.1 1.9 add_convert_fusion.3
  265.1 1.7 constant_dynamic-slice_fusion.8
  269.0 14.4 %all-gather.14.cloned.1.call-done = bf16[2,375,768]{1,2,0:T(8,128)(2,1)} async-done(((bf16[2,375,192]{1,2,0:T(8,128)(2,1)}), bf16[2,375,768]{1,2,0:T(8,128)(2,1)}) %all-gather.14.cloned.1.call-update) | async-done | bytes 1152016 | tf_op jit(solution)/shard_map/all_gather | solution.py:21
  283.4 3.4 fusion.39
  286.8 6.3 multiply_convert_fusion.1
  294.2 3.4 convolution_convert_fusion.1
  297.7 5.3 all-gather.16.cloned.1.call-done
  303.0 5.5 convert_reduce_fusion
  309.5 3.5 convolution_convert_fusion
  313.1 18.3 %reduce-scatter.8.cloned.1.call-done = bf16[2,375,192]{1,2,0:T(8,128)(2,1)} async-done(((bf16[2,375,768]{1,2,0:T(8,128)(2,1)}), bf16[2,375,192]{1,2,0:T(8,128)(2,1)}) %reduce-scatter.8.cloned.1.call-update) | async-done | bytes 288016 | tf_op jit(solution)/shard_map/reduce_scatter | solution.py:25
  331.4 28.2 %reduce-scatter.10.cloned.1.call-done = bf16[2,375,192]{1,2,0:T(8,128)(2,1)} async-done(((bf16[2,375,768]{1,2,0:T(8,128)(2,1)}), bf16[2,375,192]{1,2,0:T(8,128)(2,1)}) %reduce-scatter.10.cloned.1.call-update) | async-done | bytes 288016 | tf_op jit(solution)/shard_map/reduce_scatter | solution.py:25
  359.7 2.8 fusion.28
  362.5 6.5 all-reduce.3
  369.7 2.7 convert_reduce_fusion.6
  372.7 18.1 %all-gather.18.cloned.1.call-done = bf16[2,375,768]{1,2,0:T(8,128)(2,1)} async-done(((bf16[2,375,192]{1,2,0:T(8,128)(2,1)}), bf16[2,375,768]{1,2,0:T(8,128)(2,1)}) %all-gather.18.cloned.1.call-update) | async-done | bytes 1152016 | tf_op jit(solution)/shard_map/all_gather | solution.py:21
  390.8 2.0 convolution_convert_fusion.4
  393.6 26.9 %while.27 = (s32[]{:T(128)}, bf16[2,375,192]{1,2,0:T(8,128)(2,1)}, bf16[2,1500,192]{1,2,0:T(8,128)(2,1)}, bf16[2,1500,192]{1,2,0:T(8,128)(2,1)}, bf16[2,1500,192...) while((s32[]{:T(128)}, bf16[2,375,192]{1,2,0:T(8,128)(2,1)}, ...), condition=%wide.region_21.22_spmd, body=%wide.region_19.21_spmd.sunk | while | flops 1094218752 | bytes 117634320 | solution.py:236
  396.3 1.9 multiply_reduce_fusion.6
  398.2 2.4 multiply_convert_fusion.3
  400.6 1.9 fusion.110
  409.7 1.9 multiply_reduce_fusion.6
  411.6 2.4 multiply_convert_fusion.3
  414.0 1.9 fusion.110
  420.4 1.8 pad_maximum_fusion
  422.3 4.6 copy.108
  428.8 2.5 bitcast_convert_fusion.1
  431.4 2.2 bitcast_convert_fusion
  434.2 86.8 %all-reduce.11.cloned.1.call-done = bf16[2,1500,384]{2,0,1:T(2,128)(2,1)} async-done(((bf16[2,1500,384]{2,0,1:T(2,128)(2,1)}), bf16[2,1500,384]{2,0,1:T(2,128)(2,1)}) %all-reduce.11.cloned.1.call-update) | async-done | bytes 2304016
  521.0 1.5 constant_dynamic-slice_fusion.7
  524.3 3.1 bitcast_convert_fusion.2
  527.4 1.5 copy.112
  528.9 6.0 concatenate.38
  535.0 3.7 all-to-all-start.1
  538.8 3.6 convolution_convert_fusion.3
  542.7 43.5 %all-to-all-done.1 = bf16[4,192,2304]{2,1,0:T(8,128)(2,1)S(1)} async-done(((bf16[4,192,2304]{2,1,0:T(8,128)(2,1)}), bf16[4,192,2304]{2,1,0:T(8,128)(2,1)S(1)}, u32[]{:S(2)}, u32[]{:S(2)}) %all-to-all-start.1) | async-done | bytes 3538976 | tf_op jit(solution)/shard_map/all_to_all | solution.py:251
  586.1 2.2 copy.126
  590.7 6.0 all-reduce.2
  596.7 1.6 convert_reduce_fusion.5
  599.3 53.8 %reduce-scatter.14.cloned.1.call-done = bf16[192,2304]{1,0:T(8,128)(2,1)} async-done(((bf16[192,9216]{1,0:T(8,128)(2,1)}), bf16[192,2304]{1,0:T(8,128)(2,1)}) %reduce-scatter.14.cloned.1.call-update) | async-done | bytes 884752 | tf_op jit(solution)/shard_map/reduce_scatter | solution.py:15
  655.3 41.5 %all-reduce.1 = (f32[768]{0:T(1024)S(1)}, f32[768]{0:T(1024)S(1)}, f32[768]{0:T(1024)S(1)}, f32[768]{0:T(1024)S(1)}, f32[768]{0:T(1024)S(1)}, /*index=5*/f32[768...) all-reduce(f32[768]{0:T(1024)S(1)} %dynamic_update_slice.45, ...), channel_id=1, replica_groups=mesh['dp'=2,'row'=4,'col'=4] {'dp','row','col'}, use_global_device_ids=true, to_apply=%region_29.30 | all-reduce | flops 9216 | bytes 73728 | tf_op jit(solution)/shard_map/psum | solution.py:267
  702.6 1.9 fusion.46
  704.5 2.8 copy.116
  707.4 2.8 copy.115
  710.2 1.4 convert_element_type.139
  (279 shorter events, 48.4 us)
Async XLA Ops:
  8.0 85.2 %copy-start = (bf16[2,375,768]{2,0,1:T(2,128)(2,1)S(1)}, bf16[2,375,768]{2,0,1:T(2,128)(2,1)}, u32[]{:S(2)}) copy-start(bf16[2,375,768]{2,0,1:T(2,128)(2,1)} %param.21) | copy-start | bytes 3456004
  8.0 76.1 %all-gather.10.cloned.1.call-start = ((), (), s32[]{:S(2)}) async-start(), calls=%async_computation.8 | async-start | bytes 4423680 | tf_op jit(solution)/shard_map/all_gather | solution.py:11
  88.2 48.3 %copy-start.50 = (f32[192]{0:T(256)S(1)}, f32[192]{0:T(256)}, u32[]{:S(2)}) copy-start(f32[192]{0:T(256)} %param.22) | copy-start | bytes 2308
  88.2 48.3 %copy-start.56 = (f32[192]{0:T(256)S(1)}, f32[192]{0:T(256)}, u32[]{:S(2)}) copy-start(f32[192]{0:T(256)} %param.23) | copy-start | bytes 2308
  88.2 65.4 %all-to-all-start = ((bf16[192,4,2304]{2,0,1:T(8,128)(2,1)}), bf16[192,4,2304]{2,0,1:T(8,128)(2,1)}, u32[]{:S(2)}, u32[]{:S(2)}) async-start(bf16[192,4,2304]{2,0,1:T(8,128)(2,1)} %bitcast.172), calls=%async_computation | async-start | bytes 7077888 | tf_op jit(solution)/shard_map/all_to_all | solution.py:194
  93.1 60.5 %all-gather.8.cloned.1.call-start = ((), (), s32[]{:S(2)}) async-start(), calls=%async_computation.7 | async-start | bytes 1474560 | tf_op jit(solution)/shard_map/all_gather | solution.py:21
  94.6 275.1 %copy-start.8 = (bf16[2,375,192]{1,2,0:T(8,128)(2,1)}, bf16[2,375,192]{1,2,0:T(8,128)(2,1)S(1)}, u32[]{:S(2)}) copy-start(bf16[2,375,192]{1,2,0:T(8,128)(2,1)S(1)} %copy.119) | copy-start | bytes 864004
  137.4 70.3 %all-gather.12.cloned.1.call-start = ((), (), s32[]{:S(2)}) async-start(), calls=%async_computation.9 | async-start | bytes 2880000 | tf_op jit(solution)/shard_map/all_gather | solution.py:11
  158.0 98.1 %reduce-scatter.6.cloned.1.call-start = ((), (), s32[]{:S(2)}) async-start(), calls=%async_computation.10 | async-start | bytes 1474560 | tf_op jit(solution)/shard_map/reduce_scatter | solution.py:25
  228.6 36.4 %copy-start.18 = (bf16[2,375,192]{1,2,0:T(8,128)(2,1)}, bf16[2,375,192]{1,2,0:T(8,128)(2,1)S(1)}, u32[]{:S(2)}) copy-start(bf16[2,375,192]{1,2,0:T(8,128)(2,1)S(1)} %get-tuple-element.99) | copy-start | bytes 864004
  228.6 27.4 %copy-start.45 = (f32[192]{0:T(256)S(1)}, f32[192]{0:T(256)}, u32[]{:S(2)}) copy-start(f32[192]{0:T(256)} %param.30) | copy-start | bytes 2308
  228.7 34.4 %copy-start.47 = (f32[192]{0:T(256)S(1)}, f32[192]{0:T(256)}, u32[]{:S(2)}) copy-start(f32[192]{0:T(256)} %param.31) | copy-start | bytes 2308
  228.7 34.4 %copy-start.57 = (f32[192]{0:T(256)S(1)}, f32[192]{0:T(256)}, u32[]{:S(2)}) copy-start(f32[192]{0:T(256)} %param.32) | copy-start | bytes 2308
  231.4 52.0 %all-gather.14.cloned.1.call-start = ((), (), s32[]{:S(2)}) async-start(), calls=%async_computation.11 | async-start | bytes 1474560 | tf_op jit(solution)/shard_map/all_gather | solution.py:21
  263.1 2.0 copy-start.37
  265.0 38.0 %all-gather.16.cloned.1.call-start = ((), (), s32[]{:S(2)}) async-start(), calls=%async_computation.13 | async-start | bytes 1474560 | tf_op jit(solution)/shard_map/all_gather | solution.py:21
  268.0 63.4 %reduce-scatter.8.cloned.1.call-start = ((), (), s32[]{:S(2)}) async-start(), calls=%async_computation.12 | async-start | bytes 1474560 | tf_op jit(solution)/shard_map/reduce_scatter | solution.py:25
  286.8 6.3 copy-start.22
  297.7 62.0 %reduce-scatter.10.cloned.1.call-start = ((), (), s32[]{:S(2)}) async-start(), calls=%async_computation.14 | async-start | bytes 1474560 | tf_op jit(solution)/shard_map/reduce_scatter | solution.py:25
  309.5 50.1 %copy-start.13 = (bf16[2,375,192]{1,2,0:T(8,128)(2,1)S(1)}, bf16[2,375,192]{1,2,0:T(8,128)(2,1)}, u32[]{:S(2)}) copy-start(bf16[2,375,192]{1,2,0:T(8,128)(2,1)} %reduce-scatter.6.cloned.1.call-done) | copy-start | bytes 864004
  313.1 56.6 %copy-start.15 = (bf16[2,375,192]{1,2,0:T(8,128)(2,1)S(1)}, bf16[2,375,192]{1,2,0:T(8,128)(2,1)}, u32[]{:S(2)}) copy-start(bf16[2,375,192]{1,2,0:T(8,128)(2,1)} %copy.122) | copy-start | bytes 864004
  313.1 77.7 %all-gather.18.cloned.1.call-start = ((), (), s32[]{:S(2)}) async-start(), calls=%async_computation.15 | async-start | bytes 1474560 | tf_op jit(solution)/shard_map/all_gather | solution.py:21
  369.7 2.7 copy-start.43
  372.4 148.6 %all-reduce.11.cloned.1.call-start = ((), (), s32[]{:S(2)}) async-start(), calls=%async_computation.20 | async-start | bytes 4608000
  400.6 2.1 copy-start.2
  403.8 1.7 copy-start.33
  403.8 3.2 copy-start.24
  404.6 2.4 copy-start.4
  404.6 2.4 copy-start.6
  404.6 2.4 copy-start.11
  414.0 2.1 copy-start.2
  417.2 1.7 copy-start.33
  417.2 3.2 copy-start.24
  418.0 2.4 copy-start.4
  418.0 2.4 copy-start.6
  418.0 2.4 copy-start.11
  426.9 1.9 copy-start.58
  428.8 2.6 copy-start.36
  428.8 2.6 copy-start.59
  431.3 2.2 copy-start.19
  431.3 2.2 copy-start.29
  433.5 90.8 %copy-start.27 = (bf16[2,375,192]{1,2,0:T(8,128)(2,1)S(1)}, bf16[2,375,192]{1,2,0:T(8,128)(2,1)}, u32[]{:S(2)}) copy-start(bf16[2,375,192]{1,2,0:T(8,128)(2,1)} %get-tuple-element.101) | copy-start | bytes 864004
  535.0 51.2 %all-to-all-start.1 = ((bf16[4,192,2304]{2,1,0:T(8,128)(2,1)}), bf16[4,192,2304]{2,1,0:T(8,128)(2,1)S(1)}, u32[]{:S(2)}, u32[]{:S(2)}) async-start(bf16[4,192,2304]{2,1,0:T(8,128)(2,1)} %concatenate.38), calls=%async_computation.5 | async-start | bytes 7077888 | tf_op jit(solution)/shard_map/all_to_all | solution.py:251
  538.7 49.8 %reduce-scatter.12.cloned.1.call-start = ((), (), s32[]{:S(2)}) async-start(), calls=%async_computation.16 | async-start | bytes 1474560 | tf_op jit(solution)/shard_map/reduce_scatter | solution.py:25
  542.4 110.8 %reduce-scatter.14.cloned.1.call-start = ((), (), s32[]{:S(2)}) async-start(), calls=%async_computation.18 | async-start | bytes 4423680 | tf_op jit(solution)/shard_map/reduce_scatter | solution.py:15
  588.3 8.3 %copy-start.14 = (bf16[2,375,192]{1,2,0:T(8,128)(2,1)S(1)}, bf16[2,375,192]{1,2,0:T(8,128)(2,1)}, u32[]{:S(2)}) copy-start(bf16[2,375,192]{1,2,0:T(8,128)(2,1)} %reduce-scatter.6.cloned.1.call-done) | copy-start | bytes 864004
  588.4 8.3 %copy-start.16 = (bf16[2,375,192]{1,2,0:T(8,128)(2,1)S(1)}, bf16[2,375,192]{1,2,0:T(8,128)(2,1)}, u32[]{:S(2)}) copy-start(bf16[2,375,192]{1,2,0:T(8,128)(2,1)} %copy.122) | copy-start | bytes 864004
  588.4 8.3 %copy-start.17 = (bf16[2,375,192]{1,2,0:T(8,128)(2,1)S(1)}, bf16[2,375,192]{1,2,0:T(8,128)(2,1)}, u32[]{:S(2)}) copy-start(bf16[2,375,192]{1,2,0:T(8,128)(2,1)} %reduce-scatter.10.cloned.1.call-done) | copy-start | bytes 864004
  588.4 8.3 %copy-start.38 = (f32[2,375]{1,0:T(2,128)S(1)}, f32[2,375]{1,0:T(2,128)}, u32[]{:S(2)}) copy-start(f32[2,375]{1,0:T(2,128)} %copy-done.37) | copy-start | bytes 9004
  588.4 8.3 %copy-start.44 = (f32[2,375]{1,0:T(2,128)S(1)}, f32[2,375]{1,0:T(2,128)}, u32[]{:S(2)}) copy-start(f32[2,375]{1,0:T(2,128)} %copy-done.43) | copy-start | bytes 9004
  588.4 8.3 %copy-start.46 = (f32[192]{0:T(256)S(1)}, f32[192]{0:T(256)}, u32[]{:S(2)}) copy-start(f32[192]{0:T(256)} %param.30) | copy-start | bytes 2308
  588.4 8.3 %copy-start.48 = (f32[192]{0:T(256)S(1)}, f32[192]{0:T(256)}, u32[]{:S(2)}) copy-start(f32[192]{0:T(256)} %param.31) | copy-start | bytes 2308
  588.4 8.3 %copy-start.49 = (f32[2,375]{1,0:T(2,128)S(1)}, f32[2,375]{1,0:T(2,128)}, u32[]{:S(2)}) copy-start(f32[2,375]{1,0:T(2,128)} %get-tuple-element.274) | copy-start | bytes 9004
  588.4 9.9 %copy-start.30 = (bf16[2,375,192]{1,2,0:T(8,128)(2,1)S(1)}, bf16[2,375,192]{1,2,0:T(8,128)(2,1)}, u32[]{:S(2)}) copy-start(bf16[2,375,192]{1,2,0:T(8,128)(2,1)} %get-tuple-element.303) | copy-start | bytes 864004
  588.5 114.2 %all-gather.20.cloned.1.call-start = ((), (), s32[]{:S(2)}) async-start(), calls=%async_computation.17 | async-start | bytes 2949120 | tf_op jit(solution)/shard_map/all_gather | solution.py:21
  590.6 62.6 %copy-start.55 = (f32[768]{0:T(1024)S(1)}, f32[768]{0:T(1024)}, u32[]{:S(2)}) copy-start(f32[768]{0:T(1024)} %get-tuple-element.311) | copy-start | bytes 9220
  590.6 62.9 %copy-start.53 = (f32[192]{0:T(256)S(1)}, f32[192]{0:T(256)}, u32[]{:S(2)}) copy-start(f32[192]{0:T(256)} %get-tuple-element.229) | copy-start | bytes 2308
  590.6 63.1 %copy-start.52 = (f32[192]{0:T(256)S(1)}, f32[192]{0:T(256)}, u32[]{:S(2)}) copy-start(f32[192]{0:T(256)} %get-tuple-element.221) | copy-start | bytes 2308
  590.6 63.4 %copy-start.54 = (f32[192]{0:T(256)S(1)}, f32[192]{0:T(256)}, u32[]{:S(2)}) copy-start(f32[192]{0:T(256)} %get-tuple-element.282) | copy-start | bytes 2308
  590.7 63.6 %copy-start.21 = (bf16[2,375,384]{1,2,0:T(8,128)(2,1)S(1)}, bf16[2,375,384]{1,2,0:T(8,128)(2,1)}, u32[]{:S(2)}) copy-start(bf16[2,375,384]{1,2,0:T(8,128)(2,1)} %copy-done.20) | copy-start | bytes 1728004
  590.7 63.6 %copy-start.28 = (bf16[2,375,192]{1,2,0:T(8,128)(2,1)S(1)}, bf16[2,375,192]{1,2,0:T(8,128)(2,1)}, u32[]{:S(2)}) copy-start(bf16[2,375,192]{1,2,0:T(8,128)(2,1)} %get-tuple-element.101) | copy-start | bytes 864004
  599.3 110.9 %all-reduce.9.cloned.1.call-start = ((), (), s32[]{:S(2)}) async-start(), calls=%async_computation.19 | async-start | bytes 1769472 | tf_op jit(solution)/shard_map/psum | solution.py:255
  710.2 2.4 copy-start.12
  710.2 4.3 copy-start.1
  (30 other events, 31.4 us)
Sparse Core Ops, SparseCore 0:
  11.5 72.6 all-gather.9
  158.1 49.5 all-gather.11
  427.0 93.9 all-reduce.10
  653.3 37.3 all-reduce.8
Sparse Core Ops, SparseCore 1:
  137.5 16.1 all-gather.7
  231.5 24.4 reduce-scatter.5
  265.1 18.3 all-gather.13
  285.7 17.3 all-gather.15
  305.7 25.6 reduce-scatter.7
  334.0 25.6 reduce-scatter.9
  372.5 18.3 all-gather.17
  542.5 31.6 reduce-scatter.11
  588.6 64.5 reduce-scatter.13
  655.4 24.3 all-gather.19
where the time goes:
time: 731 us; the launch traced here: 722 us
  waiting for transfers between devices  430 us (59%)
  blocking collectives  101 us (14%)
  local copies, waits for them, and re-layouts  78.3 us (11%)
  matrix products  53.6 us (7%)
  other arithmetic  31.4 us (4%)
  between operations  17.2 us (2%)
  starting transfers between devices  9.87 us (1%)
    all_gather x2, waiting for transfers between devices, gather_cols(): return lax.all_gather(tensor, 'col', axis=1, tiled=True)  122 us
    unnamed x15, waiting for transfers between devices  87 us
    reduce_scatter x4, waiting for transfers between devices, sum_features(): lax.psum_scatter(tensor.astype(jnp.bfloat16), 'row', scatter_dimension=2,...  71.1 us
    psum x4, blocking collectives, feature_totals(): return lax.psum((first_part, second_part), 'row')  59.5 us
    reduce_scatter x1, waiting for transfers between devices, reduce_cols(): lax.psum_scatter(tensor.astype(jnp.bfloat16), 'col', scatter_dimension=1,...  53.8 us
    all_gather x5, waiting for transfers between devices, gather_features(): return lax.all_gather(tensor, 'row', axis=2, tiled=True)  52.4 us
    all_to_all x1, waiting for transfers between devices, local(): lax.all_to_all(grad_pack.astype(jnp.bfloat16), 'row', split_axis=0, conca...  43.5 us
    psum x1, blocking collectives, local(): lax.psum((place_piece(gain_one_part, row_at, row_count), place_piece(bias...  41.5 us
  transfers between devices with their start and end apart: 16, of which 12 were waited for; matrix products, arithmetic and copies ran while one was open for 8% of the time, Pallas kernels for 0%

commit v1 on v0

v1 whole, which is shorter than its diff:
```python
import functools
import jax
import jax.numpy as jnp
from jax import lax
from jax.experimental import pallas as pl
from jax.experimental.pallas import tpu as pltpu
from jax.sharding import PartitionSpec as P

HEAD = 64
VMEM_LIMIT = 48 * 1024 * 1024


def mix(first, second, first_dim, second_dim):
    return lax.dot_general(
        first,
        second,
        (((first_dim,), (second_dim,)), ((), ())),
        preferred_element_type=jnp.float32,
    )


def gather_frames(tensor):
    return lax.all_gather(tensor, "col", axis=0, tiled=True)


def reduce_frames(tensor):
    return lax.psum_scatter(
        tensor.astype(jnp.bfloat16), "col", scatter_dimension=0, tiled=True
    ).astype(jnp.float32)


def gather_rows(tensor):
    return lax.all_gather(tensor, "row", axis=0, tiled=True)


def reduce_rows(tensor):
    return lax.psum_scatter(
        tensor.astype(jnp.bfloat16), "row", scatter_dimension=0, tiled=True
    ).astype(jnp.float32)


def all_clips(tensor):
    return lax.psum(tensor.astype(jnp.bfloat16), "dp").astype(jnp.float32)


def place_piece(vector, piece_index, piece_count):
    piece_size = vector.shape[0]
    filled = jnp.zeros((piece_size * piece_count,), jnp.float32)
    return lax.dynamic_update_slice(filled, vector, (piece_index * piece_size,))


def take_piece(vector, piece_index, piece_size):
    return lax.dynamic_slice_in_dim(vector, piece_index * piece_size, piece_size)


def gelu_exact(tensor):
    return jax.nn.gelu(tensor, approximate=False)


def norm_forward(tensor, norm_gain, norm_bias):
    average = jnp.mean(tensor, axis=-1, keepdims=True)
    variance = jnp.mean(tensor * tensor, axis=-1, keepdims=True) - average * average
    inv_std = lax.rsqrt(variance + 1e-05)
    scaled = (tensor - average) * inv_std
    return ((scaled * norm_gain + norm_bias).astype(jnp.bfloat16), scaled, inv_std)


def norm_backward(gradient, scaled, inv_std, norm_gain):
    weighted = gradient * norm_gain
    first_mean = jnp.mean(weighted, axis=-1, keepdims=True)
    second_mean = jnp.mean(weighted * scaled, axis=-1, keepdims=True)
    grad_in = inv_std * (weighted - first_mean - scaled * second_mean)
    return (grad_in, jnp.sum(gradient * scaled, axis=0), jnp.sum(gradient, axis=0))


def query_tile(count):
    for tile in (256, 128, 64, 32, 16):
        if count % tile == 0:
            return tile
    return count


def attend_kernel(query_ref, key_ref, value_ref, mask_ref, out_ref, total_ref):
    heads = query_ref.shape[1] // HEAD
    queries = query_ref[...]
    mask = mask_ref[...]
    outs = []
    totals = []
    for head in range(heads):
        span = slice(head * HEAD, (head + 1) * HEAD)
        scores = mix(queries[:, span], key_ref[:, span], 1, 1) * 0.125 + mask
        highest = jnp.max(scores, axis=-1, keepdims=True)
        powers = jnp.exp(scores - highest)
        total = jnp.sum(powers, axis=-1, keepdims=True)
        probability = (powers * (1.0 / total)).astype(jnp.bfloat16)
        outs.append(mix(probability, value_ref[:, span], 1, 0))
        totals.append(highest + jnp.log(total))
    out_ref[...] = jnp.concatenate(outs, axis=1).astype(jnp.bfloat16)
    total_ref[...] = jnp.concatenate(totals, axis=1)


def attend(queries, keys, values, mask):
    count, width = queries.shape
    heads = width // HEAD
    tile = query_tile(count)
    whole = lambda step: (0, 0)
    part = lambda step: (step, 0)
    return pl.pallas_call(
        attend_kernel,
        grid=(count // tile,),
        in_specs=[
            pl.BlockSpec((tile, width), part),
            pl.BlockSpec(keys.shape, whole),
            pl.BlockSpec(values.shape, whole),
            pl.BlockSpec(mask.shape, whole),
        ],
        out_specs=[pl.BlockSpec((tile, width), part), pl.BlockSpec((tile, heads), part)],
        out_shape=[
            jax.ShapeDtypeStruct((count, width), jnp.bfloat16),
            jax.ShapeDtypeStruct((count, heads), jnp.float32),
        ],
        compiler_params=pltpu.CompilerParams(vmem_limit_bytes=VMEM_LIMIT),
        cost_estimate=pl.CostEstimate(
            flops=4 * count * keys.shape[0] * width,
            bytes_accessed=4 * (count + keys.shape[0]) * width,
            transcendentals=count * keys.shape[0] * heads,
        ),
        name="attend",
    )(queries, keys, values, mask)


def attend_back_kernel(
    query_ref,
    key_ref,
    value_ref,
    mask_ref,
    total_ref,
    grad_ref,
    d_query_ref,
    d_key_ref,
    d_value_ref,
):
    heads = query_ref.shape[1] // HEAD
    queries = query_ref[...]
    grads = grad_ref[...]
    mask = mask_ref[...]
    totals = total_ref[...]

    @pl.when(pl.program_id(0) == 0)
    def _():
        d_key_ref[...] = jnp.zeros_like(d_key_ref)
        d_value_ref[...] = jnp.zeros_like(d_value_ref)

    d_queries = []
    d_keys = []
    d_values = []
    for head in range(heads):
        span = slice(head * HEAD, (head + 1) * HEAD)
        query = queries[:, span]
        grad = grads[:, span]
        key = key_ref[:, span]
        value = value_ref[:, span]
        scores = mix(query, key, 1, 1) * 0.125 + mask
        probability = jnp.exp(scores - totals[:, head : head + 1])
        grad_prob = mix(grad, value, 1, 1)
        row_dot = jnp.sum(probability * grad_prob, axis=-1, keepdims=True)
        grad_scores = (probability * (grad_prob - row_dot)).astype(jnp.bfloat16)
        d_queries.append(mix(grad_scores, key, 1, 0) * 0.125)
        d_keys.append(mix(grad_scores, query, 0, 0) * 0.125)
        d_values.append(mix(probability.astype(jnp.bfloat16), grad, 0, 0))
    d_query_ref[...] = jnp.concatenate(d_queries, axis=1).astype(jnp.bfloat16)
    d_key_ref[...] += jnp.concatenate(d_keys, axis=1)
    d_value_ref[...] += jnp.concatenate(d_values, axis=1)


def attend_back(queries, keys, values, mask, totals, grads):
    count, width = queries.shape
    heads = width // HEAD
    tile = query_tile(count)
    whole = lambda step: (0, 0)
    part = lambda step: (step, 0)
    return pl.pallas_call(
        attend_back_kernel,
        grid=(count // tile,),
        in_specs=[
            pl.BlockSpec((tile, width), part),
            pl.BlockSpec(keys.shape, whole),
            pl.BlockSpec(values.shape, whole),
            pl.BlockSpec(mask.shape, whole),
            pl.BlockSpec((tile, heads), part),
            pl.BlockSpec((tile, width), part),
        ],
        out_specs=[
            pl.BlockSpec((tile, width), part),
            pl.BlockSpec(keys.shape, whole),
            pl.BlockSpec(values.shape, whole),
        ],
        out_shape=[
            jax.ShapeDtypeStruct((count, width), jnp.bfloat16),
            jax.ShapeDtypeStruct(keys.shape, jnp.float32),
            jax.ShapeDtypeStruct(values.shape, jnp.float32),
        ],
        compiler_params=pltpu.CompilerParams(vmem_limit_bytes=VMEM_LIMIT),
        cost_estimate=pl.CostEstimate(
            flops=10 * count * keys.shape[0] * width,
            bytes_accessed=8 * (count + keys.shape[0]) * width,
            transcendentals=count * keys.shape[0] * heads,
        ),
        name="attend_back",
    )(queries, keys, values, mask, totals, grads)


def local(
    frames,
    ln1_gain,
    ln1_bias,
    w_query,
    b_query,
    w_key,
    w_value,
    b_value,
    w_out,
    b_out,
    ln2_gain,
    ln2_bias,
    w_fc1,
    b_fc1,
    w_fc2,
    b_fc2,
    cotangent,
):
    row_count = lax.axis_size("row")
    col_count = lax.axis_size("col")
    row_at = lax.axis_index("row")
    col_at = lax.axis_index("col")
    head_width = w_query.shape[1]
    hidden_part = w_fc1.shape[1]
    clip_count, frame_count, width = frames.shape
    feature_part = width // row_count
    parts = row_count // clip_count
    slot = -(-frame_count // (parts * 64)) * 64
    padding = ((0, 0), (0, slot * parts - frame_count), (0, 0))
    clip_at = row_at // parts
    part_at = row_at % parts

    def own_frames(tensor):
        piece = lax.dynamic_slice(
            jnp.pad(tensor, padding), (clip_at, part_at * slot, 0), (1, slot, width)
        )
        return piece[0]

    def shifted(tensor, shift):
        pairs = [
            (clip * parts + part, clip * parts + (part + shift) % parts)
            for clip in range(clip_count)
            for part in range(parts)
        ]
        return lax.ppermute(tensor, "row", pairs)

    def part_mask(part):
        real = part * slot + jnp.arange(slot) < frame_count
        return jnp.tile(jnp.where(real, 0.0, -1e30).astype(jnp.float32), col_count)

    early = gather_rows(jnp.concatenate([w_query, w_key, w_value, w_out.T], axis=1))
    vectors = gather_rows(
        jnp.stack([ln1_gain, ln1_bias, ln2_gain, ln2_bias, b_out, b_fc2], axis=1)
    ).T
    gain_one, bias_one, gain_two, bias_two, bias_out, bias_last = vectors
    late = gather_rows(jnp.concatenate([w_fc1, w_fc2], axis=1))
    joint_end = 3 * head_width
    w_joint = early[:, :joint_end]
    out_rows = early[:, joint_end:]
    first_ff = late[:, :hidden_part]
    second_ff = late[:, hidden_part:]
    bias_query = take_piece(b_query, col_at, head_width)
    bias_value = take_piece(b_value, col_at, head_width)
    bias_hidden = take_piece(b_fc1, col_at, hidden_part)
    offsets = jnp.concatenate([bias_query, jnp.zeros_like(bias_query), bias_value])

    inputs_wide = own_frames(frames).astype(jnp.float32)
    cotangent_part = own_frames(cotangent)
    normed, scaled_one, inv_std_one = norm_forward(inputs_wide, gain_one, bias_one)
    normed_all = gather_frames(normed)
    cotangent_all = gather_frames(cotangent_part)
    projected = (mix(normed_all, w_joint, 1, 0) + offsets).astype(jnp.bfloat16)
    query_part = projected[:, :head_width]
    pair_part = projected[:, head_width:]
    pair_whole = jnp.concatenate(
        [pair_part] + [shifted(pair_part, shift) for shift in range(1, parts)], axis=0
    )
    mask = jnp.concatenate([part_mask((part_at - shift) % parts) for shift in range(parts)])[None]
    key_whole = pair_whole[:, :head_width]
    value_whole = pair_whole[:, head_width:]
    attended, log_total = attend(query_part, key_whole, value_whole, mask)
    branch = reduce_frames(mix(attended, out_rows, 1, 1))
    residual = inputs_wide + branch + bias_out
    normed_two, scaled_two, inv_std_two = norm_forward(residual, gain_two, bias_two)
    normed_two_all = gather_frames(normed_two)
    pre_act = mix(normed_two_all, first_ff, 1, 0) + bias_hidden
    activated, gelu_pull = jax.vjp(gelu_exact, pre_act)
    hidden = activated.astype(jnp.bfloat16)
    block_part = (residual + reduce_frames(mix(hidden, second_ff, 1, 1)) + bias_last).astype(
        jnp.bfloat16
    )
    hidden_terms = mix(cotangent_all, second_ff, 1, 0)
    d_pre = gelu_pull(hidden_terms)[0].astype(jnp.bfloat16)
    d_normed_two = reduce_frames(mix(d_pre, first_ff, 1, 1))
    grad_second = mix(cotangent_all, hidden, 0, 0)
    grad_first = mix(normed_two_all, d_pre, 0, 0)
    late_grads = all_clips(reduce_rows(jnp.concatenate([grad_first, grad_second], axis=1)))
    d_residual_norm, gain_two_part, bias_two_part = norm_backward(
        d_normed_two, scaled_two, inv_std_two, gain_two
    )
    d_residual = cotangent_part.astype(jnp.float32) + d_residual_norm
    d_branch = d_residual.astype(jnp.bfloat16)
    d_branch_all = gather_frames(d_branch)
    d_attended = mix(d_branch_all, out_rows, 1, 0).astype(jnp.bfloat16)
    d_query, key_grads, value_grads = attend_back(
        query_part, key_whole, value_whole, mask, log_total, d_attended
    )
    grad_out_rows = mix(d_branch_all, attended, 0, 0)
    pair_grads = jnp.concatenate([key_grads, value_grads], axis=1)
    held = query_part.shape[0]
    d_pair = pair_grads[:held]
    for shift in range(1, parts):
        sent = pair_grads[shift * held : (shift + 1) * held].astype(jnp.bfloat16)
        d_pair = d_pair + shifted(sent, parts - shift).astype(jnp.float32)
    d_joint = jnp.concatenate([d_query, d_pair.astype(jnp.bfloat16)], axis=1)
    d_normed = reduce_frames(mix(d_joint, w_joint, 1, 1))
    grad_joint = mix(normed_all, d_joint, 0, 0)
    early_grads = all_clips(reduce_rows(jnp.concatenate([grad_joint, grad_out_rows], axis=1)))
    d_frames_norm, gain_one_part, bias_one_part = norm_backward(
        d_normed, scaled_one, inv_std_one, gain_one
    )
    grad_part = (d_residual + d_frames_norm).astype(jnp.bfloat16)
    joint_sums = jnp.sum(d_joint, axis=0, dtype=jnp.float32)
    hidden_sums = jnp.sum(d_pre, axis=0, dtype=jnp.float32)
    featured = jnp.concatenate(
        [
            gain_one_part,
            bias_one_part,
            gain_two_part,
            bias_two_part,
            jnp.sum(d_branch, axis=0, dtype=jnp.float32),
            jnp.sum(cotangent_part, axis=0, dtype=jnp.float32),
        ]
    )
    headed = jnp.concatenate([joint_sums[:head_width], joint_sums[2 * head_width :], hidden_sums])
    sums = lax.psum(
        jnp.concatenate([featured, place_piece(headed, col_at, col_count)]), ("dp", "row", "col")
    )
    featured_sums = take_piece(
        sums[: 6 * width].reshape(6, row_count, feature_part).transpose(1, 0, 2), row_at, 1
    )[0]
    headed_sums = take_piece(sums[6 * width :], col_at, headed.shape[0])

    def whole_frames(piece):
        whole = lax.all_gather(piece, "row", axis=0, tiled=True)
        return whole.reshape(clip_count, parts * slot, width)[:, :frame_count]

    return (
        whole_frames(block_part),
        whole_frames(grad_part),
        featured_sums[0],
        featured_sums[1],
        early_grads[:, :head_width],
        headed_sums[:head_width],
        early_grads[:, head_width : 2 * head_width],
        early_grads[:, 2 * head_width : joint_end],
        headed_sums[head_width : 2 * head_width],
        early_grads[:, joint_end:].T,
        featured_sums[4],
        featured_sums[2],
        featured_sums[3],
        late_grads[:, :hidden_part],
        headed_sums[2 * head_width :],
        late_grads[:, hidden_part:],
        featured_sums[5],
    )


def solution(mesh):
    placed = (
        P("dp", "col", None),
        P("row"),
        P("row"),
        P("row", "col"),
        P(),
        P("row", "col"),
        P("row", "col"),
        P(),
        P("col", "row"),
        P("row"),
        P("row"),
        P("row"),
        P("row", "col"),
        P(),
        P("row", "col"),
        P("row"),
        P("dp", "col", None),
    )
    return jax.shard_map(
        local,
        mesh=mesh,
        in_specs=placed,
        out_specs=(
            P("dp", "col", None),
            P("dp", "col", None),
            P("row"),
            P("row"),
            P("row", "col"),
            P("col"),
            P("row", "col"),
            P("row", "col"),
            P("col"),
            P("col", "row"),
            P("row"),
            P("row"),
            P("row"),
            P("row", "col"),
            P("col"),
            P("row", "col"),
            P("row"),
        ),
        check_vma=False,
    )
```

time: 731 us -> 493 us (0.67); the launches traced: 722 us -> 492 us
  waiting for transfers between devices: 430 us -> 315 us
  blocking collectives: 101 us -> 46 us
  local copies, waits for them, and re-layouts: 78.3 us -> 33.1 us
  Pallas kernels: 0 us -> 23.5 us
  matrix products: 53.6 us -> 37.2 us
  other arithmetic: 31.4 us -> 21.3 us
  starting transfers between devices: 9.87 us -> 1.65 us
    psum x5 -> x1, blocking collectives: 101 us -> 39.7 us  [local(): lax.psum(jnp.concatenate([featured, place_piece(headed, col_at, col_count...]
    all_to_all x2 -> x0, waiting for transfers between devices: 43.5 us -> none  [the longest x1 43.5 us: local(): lax.all_to_all(grad_pack.astype(jnp.bfloat16), 'row', split_axis=0, conca...]
    unnamed x15 -> x17, waiting for transfers between devices: 87 us -> 49.9 us
    all_gather x7 -> x8, waiting for transfers between devices: 175 us -> 151 us  [the longest x4 103 us: gather_frames(): return lax.all_gather(tensor, 'col', axis=0, tiled=True)]
    pallas_call x0 -> x2, Pallas kernels: none -> 23.5 us  [the longest x1 15.2 us: attend_back(): pl.pallas_call(attend_back_kernel, grid=(count // tile,), in_specs=[pl.Bl...]
    dot_general x26 -> x12, matrix products: 53.6 us -> 37.2 us  [mix(): lax.dot_general(first, second, (((first_dim,), (second_dim,)), ((), ())),...]
    reduce_scatter x5 -> x4, waiting for transfers between devices: 125 us -> 110 us  [reduce_frames(): lax.psum_scatter(tensor.astype(jnp.bfloat16), 'col', scatter_dimension=0,...]
    while x66 -> x0, local copies, waits for them, and re-layouts: 14.8 us -> none
  transfers between devices with their start and end apart: 16 -> 17, of which waited for: 12 -> 16; matrix products, arithmetic and copies ran while one was open for 8% -> 14% of each run, Pallas kernels for 0% -> 3%
where the time goes in v1:
time: 493 us; the launch traced here: 492 us
  waiting for transfers between devices  315 us (64%)
  blocking collectives  46 us (9%)
  matrix products  37.2 us (8%)
  local copies, waits for them, and re-layouts  33.1 us (7%)
  Pallas kernels  23.5 us (5%)
  other arithmetic  21.3 us (4%)
  between operations  14.7 us (3%)
    reduce_scatter x4, waiting for transfers between devices, reduce_frames(): lax.psum_scatter(tensor.astype(jnp.bfloat16), 'col', scatter_dimension=0,...  110 us
    all_gather x4, waiting for transfers between devices, gather_frames(): return lax.all_gather(tensor, 'col', axis=0, tiled=True)  103 us
    unnamed x17, waiting for transfers between devices  49.9 us
    psum x1, blocking collectives, local(): lax.psum(jnp.concatenate([featured, place_piece(headed, col_at, col_count...  39.7 us
    dot_general x12, matrix products, mix(): lax.dot_general(first, second, (((first_dim,), (second_dim,)), ((), ())),...  37.2 us
    all_gather x2, waiting for transfers between devices, gather_rows(): return lax.all_gather(tensor, 'row', axis=0, tiled=True)  36.1 us
    unnamed x97, local copies, waits for them, and re-layouts  22.4 us
    pallas_call x1, Pallas kernels, attend_back(): pl.pallas_call(attend_back_kernel, grid=(count // tile,), in_specs=[pl.Bl...  15.2 us
  transfers between devices with their start and end apart: 17, of which 16 were waited for; matrix products, arithmetic and copies ran while one was open for 14% of the time, Pallas kernels for 3%

profile of v1, /device:TPU:0, one launch (start us, length us, event | category | flops | bytes accessed | tf_op | source)
XLA Modules:
  0.0 492.4 jit_solution(16423854371214771027)
XLA Ops:
  7.3 1.4 copy.90
  9.2 6.3 %all-gather.1 = f32[4,192,6]{1,2,0:T(8,128)S(1)} all-gather(f32[1,192,6]{1,2,0:T(8,128)S(1)} %bitcast.108), channel_id=1, replica_groups=mesh['dp'=2,'row'=4,'col'=4] {'row'}, dimensions={0}, use_global_device_ids=true | all-gather | bytes 23040 | tf_op jit(solution)/shard_map/all_gather | solution.py:33
  16.3 0.9 fusion.36
  17.4 0.9 pad_maximum_fusion.6
  18.4 0.8 dynamic_slice.22
  19.1 0.8 dynamic_slice.23
  20.0 29.6 %all-gather.11.cloned.1.call-done = bf16[768,768]{1,0:T(8,128)(2,1)} async-done(((bf16[192,768]{1,0:T(8,128)(2,1)}), bf16[768,768]{1,0:T(8,128)(2,1)}) %all-gather.11.cloned.1.call-update) | async-done | bytes 1179664 | tf_op jit(solution)/shard_map/all_gather | solution.py:23
  49.5 18.7 %all-gather.13.cloned.1.call-done = bf16[768,768]{1,0:T(8,128)(2,1)} async-done(((bf16[192,768]{1,0:T(8,128)(2,1)}), bf16[768,768]{1,0:T(8,128)(2,1)}) %all-gather.13.cloned.1.call-update) | async-done | bytes 1179664 | tf_op jit(solution)/shard_map/all_gather | solution.py:33
  68.3 2.6 add_convert_fusion.1
  71.7 1.5 collective-permute-done
  73.6 8.4 %attend.1 = (bf16[768,192]{1,0:T(8,128)(2,1)S(1)}, f32[768,3]{1,0:T(8,128)S(1)}) custom-call(bf16[768,192]{1,0:T(8,128)(2,1)S(1)} %slice.140.query_ref, bf16[1536,192]{1,0:T(8,128)(2,1)S(1)} %get-tuple-element.139.key_ref, bf16[1536,192]{1,0:T(8,128)(2,1)S(1)} %get-tuple-element.138.value_ref, f32[1,1536]{1,0:T(1,128)S(1)} %broadcast_in_dim.16.mask_ref), custom_call_target="tpu_custom_call" | custom-call | flops 905969664 | bytes 1769472 | tf_op jit(solution)/shard_map/attend/pallas_call | solution.py:108
  82.0 2.7 convolution_convert_fusion.4
  84.8 0.9 pad_maximum_fusion.5
  85.7 28.3 %reduce-scatter.11.cloned.1.call-done = bf16[192,768]{1,0:T(8,128)(2,1)} async-done(((bf16[768,768]{1,0:T(8,128)(2,1)}), bf16[192,768]{1,0:T(8,128)(2,1)}) %reduce-scatter.11.cloned.1.call-update) | async-done | bytes 294928 | tf_op jit(solution)/shard_map/reduce_scatter | solution.py:27
  114.1 1.6 fusion.52
  115.7 1.9 add_convert_fusion.3
  117.7 1.4 copy.95
  119.1 1.4 convert_reduce_fusion.4
  120.7 0.8 dynamic_slice.24
  121.5 17.4 %all-gather.17.cloned.1.call-done = bf16[768,1536]{1,0:T(8,128)(2,1)} async-done(((bf16[192,1536]{1,0:T(8,128)(2,1)}), bf16[768,1536]{1,0:T(8,128)(2,1)}) %all-gather.17.cloned.1.call-update) | async-done | bytes 2359312 | tf_op jit(solution)/shard_map/all_gather | solution.py:33
  138.9 32.5 %all-gather.15.cloned.1.call-done = bf16[768,768]{1,0:T(8,128)(2,1)} async-done(((bf16[192,768]{1,0:T(8,128)(2,1)}), bf16[768,768]{1,0:T(8,128)(2,1)}) %all-gather.15.cloned.1.call-update) | async-done | bytes 1179664 | tf_op jit(solution)/shard_map/all_gather | solution.py:23
  171.3 9.3 %multiply_convert_fusion = (bf16[768,768]{1,0:T(8,128)(2,1)}, f32[768,768]{1,0:T(8,128)}, f32[768,768]{1,0:T(8,128)}) fusion(f32[768]{0:T(1024)S(1)} %dynamic_slice.24, bf16[768,768]{1,0:T(8,128)(2,1)} %all-gather.15.cloned.1.call-done, bf16[768,1536]{1,0:T(8,128)(2,1)} %all-gather.17.cloned.1.call-done), kind=kOutput, calls=%fused_computation.7 | convolution fusion | flops 944898048 | bytes 8260608 | tf_op jit(solution)/shard_map/dot_general | solution.py:14
  180.6 22.3 %all-gather.25.cloned.1.call-done = bf16[1,768,768]{2,1,0:T(8,128)(2,1)} async-done(((bf16[1,192,768]{2,1,0:T(8,128)(2,1)}), bf16[1,768,768]{2,1,0:T(8,128)(2,1)}) %all-gather.25.cloned.1.call-update) | async-done | bytes 1179664 | tf_op jit(solution)/shard_map/all_gather | solution.py:23
  202.9 5.5 %convert_reduce_fusion = (f32[768]{0:T(1024)}, bf16[768,768]{1,0:T(8,128)(2,1)S(1)}) fusion(f32[768,768]{1,0:T(8,128)} %get-tuple-element.136, bf16[768,1536]{1,0:T(8,128)(2,1)} %all-gather.17.cloned.1.call-done, bf16[1,768,768]{2,1,0:T(8,128)(2,1)} %all-gather.25.cloned.1.call-done, f32[768,768]{1,0:T(8,128)} %get-tuple-element.161, f32[768]{0:T(1024)S(1)} %dynamic_slice.24), kind=kOutput, calls=%fused_computation.5 | convolution fusion | flops 915995904 | bytes 8263680 | tf_op jit(solution)/shard_map/dot_general | solution.py:14
  208.4 1.0 copy-done.37
  209.5 2.2 convolution_convert_fusion.2
  211.7 3.8 convolution_convert_fusion.3
  215.6 24.5 %reduce-scatter.15.cloned.1.call-done = bf16[192,768]{1,0:T(8,128)(2,1)} async-done(((bf16[768,768]{1,0:T(8,128)(2,1)}), bf16[192,768]{1,0:T(8,128)(2,1)}) %reduce-scatter.15.cloned.1.call-update) | async-done | bytes 294928 | tf_op jit(solution)/shard_map/reduce_scatter | solution.py:27
  240.1 2.3 fusion.48
  242.4 27.9 %reduce-scatter.13.cloned.1.call-done = bf16[192,768]{1,0:T(8,128)(2,1)} async-done(((bf16[768,768]{1,0:T(8,128)(2,1)}), bf16[192,768]{1,0:T(8,128)(2,1)}) %reduce-scatter.13.cloned.1.call-update) | async-done | bytes 294928 | tf_op jit(solution)/shard_map/reduce_scatter | solution.py:27
  270.4 3.4 convert_reduce_fusion.6
  274.4 2.9 convolution_convert_fusion.1
  277.3 1.2 convolution_convert_fusion
  278.5 1.6 pad_maximum_fusion
  280.0 4.3 copy.106
  284.7 18.3 %all-gather.21.cloned.1.call-done = bf16[768,768]{1,0:T(8,128)(2,1)} async-done(((bf16[192,768]{1,0:T(8,128)(2,1)}), bf16[768,768]{1,0:T(8,128)(2,1)}) %all-gather.21.cloned.1.call-update) | async-done | bytes 1179664 | tf_op jit(solution)/shard_map/all_gather | solution.py:23
  303.0 2.0 convolution_convert_fusion.8
  305.2 15.2 %attend_back.1 = (bf16[768,192]{1,0:T(8,128)(2,1)S(1)}, f32[1536,192]{1,0:T(8,128)S(1)}, f32[1536,192]{1,0:T(8,128)}) custom-call(bf16[768,192]{1,0:T(8,128)(2,1)S(1)} %slice.140.query_ref, bf16[1536,192]{1,0:T(8,128)(2,1)S(1)} %get-tuple-element.139.key_ref, bf16[1536,192]{1,0:T(8,128)(2,1)S(1)} %get-tuple-element.138.value_ref, ...), custom_call_target="tpu_custom_call" | custom-call | flops 2264924160 | bytes 3538944 | tf_op jit(solution)/shard_map/attend_back/pallas_call | solution.py:182
  320.4 1.5 fusion.9
  322.4 1.5 collective-permute-done.1
  324.3 1.2 convolution_convert_fusion.6
  325.6 1.5 copy.104
  327.1 3.4 convolution_convert_fusion.5
  330.6 1.4 slice.147
  332.0 1.9 copy.108
  334.7 23.1 %reduce-scatter.21.cloned.1.call-done = bf16[192,1536]{1,0:T(8,128)(2,1)} async-done(((bf16[768,1536]{1,0:T(8,128)(2,1)}), bf16[192,1536]{1,0:T(8,128)(2,1)}) %reduce-scatter.21.cloned.1.call-update) | async-done | bytes 589840
  357.7 2.2 copy.107
  359.9 26.1 %reduce-scatter.19.cloned.1.call-done = bf16[192,768]{1,0:T(8,128)(2,1)} async-done(((bf16[768,768]{1,0:T(8,128)(2,1)}), bf16[192,768]{1,0:T(8,128)(2,1)}) %reduce-scatter.19.cloned.1.call-update) | async-done | bytes 294928
  386.1 1.9 copy.105
  388.3 29.3 %reduce-scatter.17.cloned.1.call-done = bf16[192,768]{1,0:T(8,128)(2,1)} async-done(((bf16[768,768]{1,0:T(8,128)(2,1)}), bf16[192,768]{1,0:T(8,128)(2,1)}) %reduce-scatter.17.cloned.1.call-update) | async-done | bytes 294928 | tf_op jit(solution)/shard_map/reduce_scatter | solution.py:27
  417.6 1.4 fusion.49
  419.1 2.0 fusion.40
  421.2 39.7 %psum.21 = f32[9216]{0:T(1024)S(1)} all-reduce(f32[9216]{0:T(1024)S(1)} %constant_dynamic-update-slice_fusion), channel_id=1, replica_groups=mesh['dp'=2,'row'=4,'col'=4] {'dp','row','col'}, use_global_device_ids=true, to_apply=%region_20.21 | all-reduce | flops 9216 | bytes 73728 | tf_op jit(solution)/shard_map/psum | solution.py:349
  462.9 0.8 all-reduce.5.cloned.1.call-done
  463.7 1.2 fusion.57
  464.9 1.1 copy.101
  466.0 1.1 copy.102
  467.2 0.8 copy.100
  468.0 0.8 copy.98
  468.8 0.8 copy.99
  469.6 0.7 slice_bitcast_fusion
  470.3 12.4 %all-gather.23.cloned.1.call-done = bf16[768,768]{1,0:T(8,128)(2,1)} async-done(((bf16[192,768]{1,0:T(8,128)(2,1)}), bf16[768,768]{1,0:T(8,128)(2,1)}) %all-gather.23.cloned.1.call-update) | async-done | bytes 1179664 | tf_op jit(solution)/shard_map/all_gather | solution.py:358
  482.7 1.3 slice.150
  484.0 1.9 copy.109
  (158 shorter events, 8.7 us)
Async XLA Ops:
  7.2 42.3 %all-gather.11.cloned.1.call-start = ((), (), s32[]{:S(2)}) async-start(), calls=%async_computation.6 | async-start | bytes 1474560 | tf_op jit(solution)/shard_map/all_gather | solution.py:23
  7.3 1.9 copy-start.27
  7.3 1.9 copy-start.28
  7.3 1.9 copy-start.29
  7.3 1.9 copy-start.30
  7.3 1.9 copy-start.31
  7.3 1.9 copy-start.32
  8.7 8.5 %copy-start = (bf16[2,375,768]{2,1,0:T(8,128)(2,1)}, bf16[2,375,768]{2,1,0:T(8,128)(2,1)S(1)}, u32[]{:S(2)}) copy-start(bf16[2,375,768]{2,1,0:T(8,128)(2,1)S(1)} %copy.90) | copy-start | bytes 3456004
  8.8 8.5 %copy-start.11 = (bf16[192,192]{1,0:T(8,128)(2,1)S(1)}, bf16[192,192]{1,0:T(8,128)(2,1)}, u32[]{:S(2)}) copy-start(bf16[192,192]{1,0:T(8,128)(2,1)} %param.25) | copy-start | bytes 221188
  8.8 8.6 %copy-start.12 = (bf16[192,192]{1,0:T(8,128)(2,1)S(1)}, bf16[192,192]{1,0:T(8,128)(2,1)}, u32[]{:S(2)}) copy-start(bf16[192,192]{1,0:T(8,128)(2,1)} %param.23) | copy-start | bytes 221188
  8.8 8.6 %copy-start.13 = (bf16[192,192]{1,0:T(8,128)(2,1)S(1)}, bf16[192,192]{1,0:T(8,128)(2,1)}, u32[]{:S(2)}) copy-start(bf16[192,192]{1,0:T(8,128)(2,1)} %param.22) | copy-start | bytes 221188
  8.8 8.6 %copy-start.14 = (bf16[192,192]{1,0:T(8,128)(2,1)S(1)}, bf16[192,192]{1,0:T(8,128)(2,1)}, u32[]{:S(2)}) copy-start(bf16[192,192]{1,0:T(8,128)(2,1)} %param.20) | copy-start | bytes 221188
  16.3 33.2 %copy-start.16 = (f32[192]{0:T(256)}, f32[192]{0:T(256)S(1)}, u32[]{:S(2)}) copy-start(f32[192]{0:T(256)S(1)} %get-tuple-element.159) | copy-start | bytes 2308
  16.3 33.2 %copy-start.18 = (f32[192]{0:T(256)}, f32[192]{0:T(256)S(1)}, u32[]{:S(2)}) copy-start(f32[192]{0:T(256)S(1)} %get-tuple-element.160) | copy-start | bytes 2308
  17.2 51.0 %all-gather.13.cloned.1.call-start = ((), (), s32[]{:S(2)}) async-start(), calls=%async_computation.7 | async-start | bytes 1474560 | tf_op jit(solution)/shard_map/all_gather | solution.py:33
  18.3 95.8 %reduce-scatter.11.cloned.1.call-start = ((), (), s32[]{:S(2)}) async-start(), calls=%async_computation.8 | async-start | bytes 1474560 | tf_op jit(solution)/shard_map/reduce_scatter | solution.py:27
  71.2 2.1 collective-permute-start
  82.0 2.8 copy-start.9
  82.0 2.8 copy-start.10
  84.7 31.0 %copy-start.15 = (f32[768]{0:T(1024)S(1)}, f32[768]{0:T(1024)}, u32[]{:S(2)}) copy-start(f32[768]{0:T(1024)} %get-tuple-element.124) | copy-start | bytes 9220
  84.7 31.0 %copy-start.25 = (f32[768]{0:T(1024)S(1)}, f32[768]{0:T(1024)}, u32[]{:S(2)}) copy-start(f32[768]{0:T(1024)} %get-tuple-element.123) | copy-start | bytes 9220
  84.7 54.1 %all-gather.17.cloned.1.call-start = ((), (), s32[]{:S(2)}) async-start(), calls=%async_computation.10 | async-start | bytes 2949120 | tf_op jit(solution)/shard_map/all_gather | solution.py:33
  85.7 85.7 %all-gather.15.cloned.1.call-start = ((), (), s32[]{:S(2)}) async-start(), calls=%async_computation.9 | async-start | bytes 1474560 | tf_op jit(solution)/shard_map/all_gather | solution.py:23
  114.1 1.6 copy-start.1
  117.6 85.3 %all-gather.25.cloned.1.call-start = ((), (), s32[]{:S(2)}) async-start(), calls=%async_computation.17 | async-start | bytes 1474560 | tf_op jit(solution)/shard_map/all_gather | solution.py:23
  120.5 119.6 %reduce-scatter.15.cloned.1.call-start = ((), (), s32[]{:S(2)}) async-start(), calls=%async_computation.13 | async-start | bytes 1474560 | tf_op jit(solution)/shard_map/reduce_scatter | solution.py:27
  202.9 6.5 %copy-start.33 = (bf16[768,1536]{1,0:T(8,128)(2,1)S(1)}, bf16[768,1536]{1,0:T(8,128)(2,1)}, u32[]{:S(2)}) copy-start(bf16[768,1536]{1,0:T(8,128)(2,1)} %all-gather.17.cloned.1.call-done) | copy-start | bytes 7077892
  208.4 1.0 copy-start.37
  211.6 58.7 %reduce-scatter.13.cloned.1.call-start = ((), (), s32[]{:S(2)}) async-start(), calls=%async_computation.11 | async-start | bytes 1474560 | tf_op jit(solution)/shard_map/reduce_scatter | solution.py:27
  211.7 28.4 %copy-start.5 = (bf16[192,768]{1,0:T(8,128)(2,1)S(1)}, bf16[192,768]{1,0:T(8,128)(2,1)}, u32[]{:S(2)}) copy-start(bf16[192,768]{1,0:T(8,128)(2,1)} %reduce-scatter.11.cloned.1.call-done) | copy-start | bytes 884740
  215.5 54.8 %copy-start.6 = (bf16[1,192,768]{2,1,0:T(8,128)(2,1)S(1)}, bf16[1,192,768]{2,1,0:T(8,128)(2,1)}, u32[]{:S(2)}) copy-start(bf16[1,192,768]{2,1,0:T(8,128)(2,1)} %get-tuple-element.131) | copy-start | bytes 884740
  215.5 54.8 %copy-start.24 = (f32[768]{0:T(1024)S(1)}, f32[768]{0:T(1024)}, u32[]{:S(2)}) copy-start(f32[768]{0:T(1024)} %get-tuple-element.122) | copy-start | bytes 9220
  215.5 87.5 %all-gather.21.cloned.1.call-start = ((), (), s32[]{:S(2)}) async-start(), calls=%async_computation.14 | async-start | bytes 1474560 | tf_op jit(solution)/shard_map/all_gather | solution.py:23
  273.7 56.9 %all-gather.19.cloned.1.call-start = ((), (), s32[]{:S(2)}) async-start(), calls=%async_computation.12 | async-start | bytes 1474560 | tf_op jit(solution)/shard_map/all_gather | solution.py:358
  274.3 83.4 %reduce-scatter.21.cloned.1.call-start = ((), (), s32[]{:S(2)}) async-start(), calls=%async_computation.19 | async-start | bytes 2949120
  274.4 2.9 copy-start.35
  274.4 2.9 copy-start.36
  284.4 101.6 %reduce-scatter.19.cloned.1.call-start = ((), (), s32[]{:S(2)}) async-start(), calls=%async_computation.18 | async-start | bytes 1474560
  320.4 1.6 copy-start.4
  320.4 3.6 copy-start.3
  321.9 2.1 collective-permute-start.1
  322.4 1.8 copy-start.34
  327.1 90.5 %reduce-scatter.17.cloned.1.call-start = ((), (), s32[]{:S(2)}) async-start(), calls=%async_computation.15 | async-start | bytes 1474560 | tf_op jit(solution)/shard_map/reduce_scatter | solution.py:27
  330.5 133.2 %all-reduce.5.cloned.1.call-start = ((), (), s32[]{:S(2)}) async-start(), calls=%async_computation.20 | async-start | bytes 2359296 | tf_op jit(solution)/shard_map/psum | solution.py:43
  332.0 2.3 copy-start.26
  333.9 83.7 %copy-start.2 = (bf16[2,375,768]{2,1,0:T(8,128)(2,1)S(1)}, bf16[2,375,768]{2,1,0:T(8,128)(2,1)}, u32[]{:S(2)}) copy-start(bf16[2,375,768]{2,1,0:T(8,128)(2,1)} %copy-done) | copy-start | bytes 3456004
  333.9 83.7 %copy-start.17 = (f32[192]{0:T(256)S(1)}, f32[192]{0:T(256)}, u32[]{:S(2)}) copy-start(f32[192]{0:T(256)} %copy-done.16) | copy-start | bytes 2308
  333.9 83.7 %copy-start.19 = (f32[192]{0:T(256)S(1)}, f32[192]{0:T(256)}, u32[]{:S(2)}) copy-start(f32[192]{0:T(256)} %copy-done.18) | copy-start | bytes 2308
  359.9 59.1 %copy-start.23 = (f32[768]{0:T(1024)S(1)}, f32[768]{0:T(1024)}, u32[]{:S(2)}) copy-start(f32[768]{0:T(1024)} %get-tuple-element.112) | copy-start | bytes 9220
  359.9 59.1 %copy-start.22 = (f32[768]{0:T(1024)S(1)}, f32[768]{0:T(1024)}, u32[]{:S(2)}) copy-start(f32[768]{0:T(1024)} %get-tuple-element.120) | copy-start | bytes 9220
  359.9 59.2 %copy-start.8 = (f32[192,768]{1,0:T(8,128)S(1)}, f32[192,768]{1,0:T(8,128)}, u32[]{:S(2)}) copy-start(f32[192,768]{1,0:T(8,128)} %get-tuple-element.134) | copy-start | bytes 1769476
  388.0 33.1 %copy-start.21 = (f32[768]{0:T(1024)S(1)}, f32[768]{0:T(1024)}, u32[]{:S(2)}) copy-start(f32[768]{0:T(1024)} %get-tuple-element.132) | copy-start | bytes 9220
  388.0 33.2 %copy-start.20 = (f32[768]{0:T(1024)S(1)}, f32[768]{0:T(1024)}, u32[]{:S(2)}) copy-start(f32[768]{0:T(1024)} %get-tuple-element.130) | copy-start | bytes 9220
  388.0 94.7 %all-gather.23.cloned.1.call-start = ((), (), s32[]{:S(2)}) async-start(), calls=%async_computation.16 | async-start | bytes 1474560 | tf_op jit(solution)/shard_map/all_gather | solution.py:358
  464.9 2.1 copy-start.7
Sparse Core Ops, SparseCore 0:
  17.3 32.1 all-gather.10
  51.7 16.5 all-gather.12
  84.8 29.1 reduce-scatter.10
  116.1 22.7 all-gather.16
  140.9 30.4 all-gather.14
  173.3 29.5 all-gather.24
  211.8 28.2 reduce-scatter.14
  242.4 27.8 reduce-scatter.12
  273.9 29.1 all-gather.20
  305.0 16.5 all-gather.18
  324.2 33.5 reduce-scatter.20
  360.3 25.7 reduce-scatter.18
  388.4 29.1 reduce-scatter.16
  420.9 42.7 all-reduce.4
  465.2 17.4 all-gather.22

commit v2 on v1

v2 whole, which is shorter than its diff:
```python
import functools
import jax
import jax.numpy as jnp
from jax import lax
from jax.experimental import pallas as pl
from jax.experimental.pallas import tpu as pltpu
from jax.sharding import PartitionSpec as P

HEAD = 64
VMEM_LIMIT = 48 * 1024 * 1024


def mix(first, second, first_dim, second_dim):
    return lax.dot_general(
        first,
        second,
        (((first_dim,), (second_dim,)), ((), ())),
        preferred_element_type=jnp.float32,
    )


def gather_rows(tensor):
    return lax.all_gather(tensor, "row", axis=0, tiled=True)


def reduce_rows(tensor):
    return lax.psum_scatter(
        tensor.astype(jnp.bfloat16), "row", scatter_dimension=0, tiled=True
    ).astype(jnp.float32)


def all_clips(tensor):
    return lax.psum(tensor.astype(jnp.bfloat16), "dp").astype(jnp.float32)


def place_piece(vector, piece_index, piece_count):
    piece_size = vector.shape[0]
    filled = jnp.zeros((piece_size * piece_count,), jnp.float32)
    return lax.dynamic_update_slice(filled, vector, (piece_index * piece_size,))


def take_piece(vector, piece_index, piece_size):
    return lax.dynamic_slice_in_dim(vector, piece_index * piece_size, piece_size)


def put(src, dst, send, recv, axis, index):
    return pltpu.make_async_remote_copy(
        src_ref=src,
        dst_ref=dst,
        send_sem=send,
        recv_sem=recv,
        device_id={axis: index},
        device_id_type=pl.DeviceIdType.MESH,
    )


def ring(me, step, count):
    return lax.rem(me + step, count)


def span(index, size):
    return pl.ds(pl.multiple_of(index * size, size), size)


class Gather:
    def __init__(self, axis, count, source, whole, sends, recvs, row):
        self.axis, self.count, self.me = axis, count, lax.axis_index(axis)
        self.source, self.whole, self.row = source, whole, row
        self.sends, self.recvs = sends, recvs

    def copy(self, step):
        size = self.source.shape[0]
        return put(
            self.source,
            self.whole.at[span(self.me, size)],
            self.sends.at[self.row, step - 1],
            self.recvs.at[self.row, step - 1],
            self.axis,
            ring(self.me, step, self.count),
        )

    def start(self):
        for step in range(1, self.count):
            self.copy(step).start()

    def keep_own(self):
        self.whole[span(self.me, self.source.shape[0]), :] = self.source[...]

    def wait(self):
        for step in range(1, self.count):
            self.copy(step).wait_recv()

    def finish(self):
        for step in range(1, self.count):
            self.copy(step).wait_send()


class Reduce:
    def __init__(self, axis, count, outgoing, incoming, sends, recvs, row, toward=1):
        self.axis, self.count, self.me = axis, count, lax.axis_index(axis)
        self.outgoing, self.incoming, self.row = outgoing, incoming, row
        self.sends, self.recvs, self.toward = sends, recvs, toward

    def copy(self, step):
        ahead = step if self.toward > 0 else self.count - step
        return put(
            self.outgoing.at[step - 1],
            self.incoming.at[step - 1],
            self.sends.at[self.row, step - 1],
            self.recvs.at[self.row, step - 1],
            self.axis,
            ring(self.me, ahead, self.count),
        )

    def send(self, step, value):
        self.outgoing[step - 1] = value.astype(self.outgoing.dtype)
        self.copy(step).start()

    def total(self, own):
        for step in range(1, self.count):
            self.copy(step).wait_recv()
            own = own + self.incoming[step - 1].astype(jnp.float32)
        return own

    def finish(self):
        for step in range(1, self.count):
            self.copy(step).wait_send()


def greet(peers):
    barrier = pltpu.get_barrier_semaphore()
    for axis, index in peers:
        pl.semaphore_signal(
            barrier, inc=1, device_id={axis: index}, device_id_type=pl.DeviceIdType.MESH
        )
    pl.semaphore_wait(barrier, len(peers))


def others(axis, count):
    me = lax.axis_index(axis)
    return [(axis, ring(me, step, count)) for step in range(1, count)]


def partner_row():
    me = lax.axis_index("row")
    return me + 1 - 2 * lax.rem(me, 2)


def norm_stats(tensor):
    average = jnp.mean(tensor, axis=-1, keepdims=True)
    variance = jnp.mean(tensor * tensor, axis=-1, keepdims=True) - average * average
    inv_std = lax.rsqrt(variance + 1e-05)
    return (tensor - average) * inv_std, inv_std


def norm_backward(gradient, scaled, inv_std, norm_gain):
    weighted = gradient * norm_gain
    first_mean = jnp.mean(weighted, axis=-1, keepdims=True)
    second_mean = jnp.mean(weighted * scaled, axis=-1, keepdims=True)
    return inv_std * (weighted - first_mean - scaled * second_mean)


def column_sums(tensor):
    return jnp.sum(tensor, axis=0, keepdims=True)


def front_kernel(
    n_row, n_col,
    x_ref, vec_ref, wq_ref, wkv_ref, wo_ref, bq_ref, bkv_ref, mask_ref,
    vec_out, wq_out, wkv_out, wo_out, normed_out, query_out, pair_out, att_out, total_out,
    resid_out, normed2_out,
    vec_buf, wq_buf, wkv_buf, wo_buf, own_buf, normed_buf, pair_buf, away_buf, sum_out, sum_in,
    own_sum, sends, recvs, pair_sends, pair_recvs,
):
    slot = x_ref.shape[0]
    head_width = wq_ref.shape[1]
    held = slot * n_col
    col_at = lax.axis_index("col")
    partner = partner_row()
    greet(others("row", n_row) + others("col", n_col))
    vec = Reduce("row", n_row, None, vec_buf, sends, recvs, 0)
    vec_copies = [
        put(vec_ref, vec_buf.at[step - 1], sends.at[0, step - 1], recvs.at[0, step - 1], "row",
            ring(vec.me, step, n_row))
        for step in range(1, n_row)
    ]
    for copy in vec_copies:
        copy.start()
    gathers = [
        Gather("row", n_row, wq_ref, wq_buf, sends, recvs, 1),
        Gather("row", n_row, wkv_ref, wkv_buf, sends, recvs, 2),
        Gather("row", n_row, wo_ref, wo_buf, sends, recvs, 3),
    ]
    for gather in gathers:
        gather.start()
    scaled, _ = norm_stats(x_ref[...].astype(jnp.float32))
    vectors = vec_ref[...]
    for step, copy in enumerate(vec_copies):
        copy.wait_recv()
        vectors = vectors + vec_buf[step]
    vec_out[...] = vectors
    own_buf[...] = (scaled * vectors[0:1] + vectors[1:2]).astype(jnp.bfloat16)
    frames = Gather("col", n_col, own_buf, normed_buf, sends, recvs, 4)
    frames.start()
    frames.keep_own()
    for gather in gathers:
        gather.keep_own()
    for gather in gathers:
        gather.wait()

    def pair_copy(at):
        return put(
            pair_buf.at[span(at, slot)],
            away_buf.at[span(at, slot)],
            pair_sends.at[at],
            pair_recvs.at[at],
            "row",
            partner,
        )

    def project(step, carry):
        sender = ring(col_at, n_col - step, n_col)

        @pl.when(step > 0)
        def _():
            frames.copy(step).wait_recv()

        block = normed_buf[span(sender, slot), :]
        normed_out[span(sender, slot), :] = block
        query_out[span(sender, slot), :] = (
            mix(block, wq_buf[...], 1, 0) + bq_ref[...]
        ).astype(jnp.bfloat16)
        pair_buf[span(sender, slot), :] = (
            mix(block, wkv_buf[...], 1, 0) + bkv_ref[...]
        ).astype(jnp.bfloat16)
        pair_copy(sender).start()
        return carry

    lax.fori_loop(0, n_col, project, 0)
    for at in range(n_col):
        pair_copy(at).wait_recv()
    pair_out[0:held, :] = pair_buf[...]
    pair_out[held : 2 * held, :] = away_buf[...]
    sums = Reduce("col", n_col, sum_out, sum_in, sends, recvs, 5)
    mask = mask_ref[...]

    def attend(step, carry):
        owner = ring(col_at, step, n_col)
        queries = query_out[span(owner, slot), :]
        outs = []
        totals = []
        for head in range(head_width // HEAD):
            low = head * HEAD
            key = pair_out[:, low : low + HEAD]
            value = pair_out[:, head_width + low : head_width + low + HEAD]
            scores = mix(queries[:, low : low + HEAD], key, 1, 1) * 0.125 + mask
            highest = jnp.max(scores, axis=-1, keepdims=True)
            powers = jnp.exp(scores - highest)
            total = jnp.sum(powers, axis=-1, keepdims=True)
            probability = (powers * (1.0 / total)).astype(jnp.bfloat16)
            outs.append(mix(probability, value, 1, 0))
            totals.append(highest + jnp.log(total))
        attended = jnp.concatenate(outs, axis=1).astype(jnp.bfloat16)
        att_out[span(owner, slot), :] = attended
        total_out[span(owner, slot), :] = jnp.concatenate(totals, axis=1)
        partial = mix(attended, wo_buf[...], 1, 1)

        @pl.when(step < n_col)
        def _():
            sums.send(step, partial)

        @pl.when(step == n_col)
        def _():
            own_sum[...] = partial

        return carry

    lax.fori_loop(1, n_col + 1, attend, 0)
    wq_out[...] = wq_buf[...]
    wkv_out[...] = wkv_buf[...]
    wo_out[...] = wo_buf[...]
    residual = x_ref[...].astype(jnp.float32) + sums.total(own_sum[...]) + vectors[4:5]
    resid_out[...] = residual
    scaled, _ = norm_stats(residual)
    normed2_out[...] = (scaled * vectors[2:3] + vectors[3:4]).astype(jnp.bfloat16)
    for copy in vec_copies:
        copy.wait_send()
    for gather in gathers:
        gather.finish()
    frames.finish()
    for at in range(n_col):
        pair_copy(at).wait_send()
    sums.finish()


def middle_kernel(
    n_col,
    normed2_ref, resid_ref, cot_ref, cot_all_ref, w1_ref, w2_ref, vec_ref, bh_ref,
    block_out, d_branch_out, d_resid_out, g1_out, g2_out, small_out, hidden_sum_out,
    normed_buf, hidden_buf, d_pre_buf, d_own, d_buf, sum_out, sum_in, own_sum, last_out, last_in,
    own_last, sends, recvs,
):
    slot = resid_ref.shape[0]
    col_at = lax.axis_index("col")
    greet(others("col", n_col))
    frames = Gather("col", n_col, normed2_ref, normed_buf, sends, recvs, 0)
    frames.start()
    frames.keep_own()
    sums = Reduce("col", n_col, sum_out, sum_in, sends, recvs, 1, -1)
    lasts = Reduce("col", n_col, last_out, last_in, sends, recvs, 2, -1)

    def feed(step, carry):
        sender = ring(col_at, n_col - step, n_col)

        @pl.when(step > 0)
        def _():
            frames.copy(step).wait_recv()

        block = normed_buf[span(sender, slot), :]
        pre = mix(block, w1_ref[...], 1, 0) + bh_ref[...]
        normal = 0.5 * (1.0 + lax.erf(pre * 0.7071067811865476))
        hidden = (pre * normal).astype(jnp.bfloat16)
        hidden_buf[span(sender, slot), :] = hidden
        slope = normal + pre * (0.3989422804014327 * jnp.exp(-0.5 * pre * pre))
        terms = mix(cot_all_ref[span(sender, slot), :], w2_ref[...], 1, 0)
        d_pre = (terms * slope).astype(jnp.bfloat16)
        d_pre_buf[span(sender, slot), :] = d_pre
        partial = mix(d_pre, w1_ref[...], 1, 1)

        @pl.when(step > 0)
        def _():
            sums.send(step, partial)

        @pl.when(step == 0)
        def _():
            own_sum[...] = partial

        return carry

    lax.fori_loop(0, n_col, feed, 0)
    scaled, inv_std = norm_stats(resid_ref[...])
    d_normed = sums.total(own_sum[...])
    d_resid = cot_ref[...].astype(jnp.float32) + norm_backward(
        d_normed, scaled, inv_std, vec_ref[2:3, :]
    )
    d_resid_out[...] = d_resid
    d_own[...] = d_resid.astype(jnp.bfloat16)
    backs = Gather("col", n_col, d_own, d_buf, sends, recvs, 3)
    backs.start()
    backs.keep_own()
    def finish_block(step, carry):
        sender = ring(col_at, n_col - step, n_col)
        partial = mix(hidden_buf[span(sender, slot), :], w2_ref[...], 1, 1)

        @pl.when(step > 0)
        def _():
            lasts.send(step, partial)

        @pl.when(step == 0)
        def _():
            own_last[...] = partial

        return carry

    lax.fori_loop(0, n_col, finish_block, 0)
    g1_out[...] = mix(normed_buf[...], d_pre_buf[...], 0, 0).astype(jnp.bfloat16)
    g2_out[...] = mix(cot_all_ref[...], hidden_buf[...], 0, 0).astype(jnp.bfloat16)
    hidden_sum_out[...] = column_sums(d_pre_buf[...].astype(jnp.float32))
    small_out[...] = jnp.concatenate(
        [
            column_sums(d_normed * scaled),
            column_sums(d_normed),
            column_sums(d_own[...].astype(jnp.float32)),
            column_sums(cot_ref[...].astype(jnp.float32)),
        ],
        axis=0,
    )
    backs.wait()
    d_branch_out[...] = d_buf[...]
    block_out[...] = (
        resid_ref[...] + lasts.total(own_last[...]) + vec_ref[5:6, :]
    ).astype(jnp.bfloat16)
    frames.finish()
    sums.finish()
    lasts.finish()
    backs.finish()


def back_kernel(
    n_col,
    x_ref, d_resid_ref, vec_ref, wq_ref, wkv_ref, wo_ref, normed_ref, query_ref, pair_ref,
    att_ref, total_ref, mask_ref, d_branch_ref,
    frames_out, small_out, bq_out, bkv_out, gq_out, gkv_out, go_out,
    d_query_buf, d_key_buf, d_value_buf, pair_buf, away_buf, d_pair_buf, sum_out, sum_in, own_sum,
    sends, recvs, pair_sends, pair_recvs,
):
    slot = x_ref.shape[0]
    head_width = wq_ref.shape[1]
    held = slot * n_col
    col_at = lax.axis_index("col")
    partner = partner_row()
    greet([("row", partner)] + others("col", n_col))
    d_key_buf[...] = jnp.zeros_like(d_key_buf)
    d_value_buf[...] = jnp.zeros_like(d_value_buf)
    mask = mask_ref[...]

    def attend_back(at, carry):
        grads = mix(d_branch_ref[span(at, slot), :], wo_ref[...], 1, 0).astype(jnp.bfloat16)
        queries = query_ref[span(at, slot), :]
        totals = total_ref[span(at, slot), :]
        d_queries = []
        d_keys = []
        d_values = []
        for head in range(head_width // HEAD):
            low = head * HEAD
            query = queries[:, low : low + HEAD]
            grad = grads[:, low : low + HEAD]
            key = pair_ref[:, low : low + HEAD]
            value = pair_ref[:, head_width + low : head_width + low + HEAD]
            scores = mix(query, key, 1, 1) * 0.125 + mask
            probability = jnp.exp(scores - totals[:, head : head + 1])
            grad_prob = mix(grad, value, 1, 1)
            row_dot = jnp.sum(probability * grad_prob, axis=-1, keepdims=True)
            grad_scores = (probability * (grad_prob - row_dot)).astype(jnp.bfloat16)
            d_queries.append(mix(grad_scores, key, 1, 0) * 0.125)
            d_keys.append(mix(grad_scores, query, 0, 0) * 0.125)
            d_values.append(mix(probability.astype(jnp.bfloat16), grad, 0, 0))
        d_query_buf[span(at, slot), :] = jnp.concatenate(d_queries, axis=1).astype(jnp.bfloat16)
        d_key_buf[...] += jnp.concatenate(d_keys, axis=1)
        d_value_buf[...] += jnp.concatenate(d_values, axis=1)
        return carry

    lax.fori_loop(0, n_col, attend_back, 0)
    pair_buf[0] = d_key_buf[held : 2 * held, :].astype(jnp.bfloat16)
    pair_buf[1] = d_value_buf[held : 2 * held, :].astype(jnp.bfloat16)
    crossing = put(pair_buf, away_buf, pair_sends.at[0], pair_recvs.at[0], "row", partner)
    crossing.start()
    gq_out[...] = mix(normed_ref[...], d_query_buf[...], 0, 0).astype(jnp.bfloat16)
    go_out[...] = mix(d_branch_ref[...], att_ref[...], 0, 0).astype(jnp.bfloat16)
    crossing.wait_recv()
    d_key = d_key_buf[0:held, :] + away_buf[0].astype(jnp.float32)
    d_value = d_value_buf[0:held, :] + away_buf[1].astype(jnp.float32)
    d_pair_buf[...] = jnp.concatenate([d_key, d_value], axis=1).astype(jnp.bfloat16)
    sums = Reduce("col", n_col, sum_out, sum_in, sends, recvs, 0)

    def spread(step, carry):
        owner = ring(col_at, step, n_col)
        partial = mix(d_query_buf[span(owner, slot), :], wq_ref[...], 1, 1) + mix(
            d_pair_buf[span(owner, slot), :], wkv_ref[...], 1, 1
        )

        @pl.when(step < n_col)
        def _():
            sums.send(step, partial)

        @pl.when(step == n_col)
        def _():
            own_sum[...] = partial

        return carry

    lax.fori_loop(1, n_col + 1, spread, 0)
    gkv_out[...] = mix(normed_ref[...], d_pair_buf[...], 0, 0).astype(jnp.bfloat16)
    bq_out[...] = column_sums(d_query_buf[...].astype(jnp.float32))
    bkv_out[...] = column_sums(d_pair_buf[...].astype(jnp.float32))
    scaled, inv_std = norm_stats(x_ref[...].astype(jnp.float32))
    d_normed = sums.total(own_sum[...])
    frames_out[...] = (
        d_resid_ref[...] + norm_backward(d_normed, scaled, inv_std, vec_ref[0:1, :])
    ).astype(jnp.bfloat16)
    small_out[...] = jnp.concatenate(
        [column_sums(d_normed * scaled), column_sums(d_normed)], axis=0
    )
    crossing.wait_send()
    sums.finish()


def call(kernel, name, number, flops, outs, scratch, *operands):
    return pl.pallas_call(
        kernel,
        in_specs=[pl.BlockSpec(memory_space=pltpu.VMEM)] * len(operands),
        out_specs=[pl.BlockSpec(memory_space=pltpu.VMEM)] * len(outs),
        out_shape=[jax.ShapeDtypeStruct(shape, kind) for shape, kind in outs],
        scratch_shapes=scratch,
        compiler_params=pltpu.CompilerParams(
            vmem_limit_bytes=VMEM_LIMIT, collective_id=number, has_side_effects=True
        ),
        cost_estimate=pl.CostEstimate(flops=flops, bytes_accessed=60000000, transcendentals=0),
        name=name,
    )(*operands)


def local(
    frames,
    ln1_gain,
    ln1_bias,
    w_query,
    b_query,
    w_key,
    w_value,
    b_value,
    w_out,
    b_out,
    ln2_gain,
    ln2_bias,
    w_fc1,
    b_fc1,
    w_fc2,
    b_fc2,
    cotangent,
):
    row_count = lax.axis_size("row")
    col_count = lax.axis_size("col")
    row_at = lax.axis_index("row")
    col_at = lax.axis_index("col")
    head_width = w_query.shape[1]
    hidden_part = w_fc1.shape[1]
    clip_count, frame_count, width = frames.shape
    feature_part = width // row_count
    parts = row_count // clip_count
    slot = -(-frame_count // (parts * 64)) * 64
    padding = ((0, 0), (0, slot * parts - frame_count), (0, 0))
    clip_at = row_at // parts
    part_at = row_at % parts

    def own_frames(tensor):
        piece = lax.dynamic_slice(
            jnp.pad(tensor, padding), (clip_at, part_at * slot, 0), (1, slot, width)
        )
        return piece[0]

    def part_mask(part):
        real = part * slot + jnp.arange(slot) < frame_count
        return jnp.tile(jnp.where(real, 0.0, -1e30).astype(jnp.float32), col_count)

    bf16, f32 = jnp.bfloat16, jnp.float32
    held = slot * col_count
    away = max(row_count, col_count) - 1
    dma = pltpu.SemaphoreType.DMA
    late = gather_rows(jnp.concatenate([w_fc1, w_fc2], axis=1))
    bias_query = take_piece(b_query, col_at, head_width)
    bias_value = take_piece(b_value, col_at, head_width)
    bias_hidden = take_piece(b_fc1, col_at, hidden_part)
    bias_pair = jnp.concatenate([jnp.zeros_like(bias_value), bias_value])
    stacked = jnp.stack(
        [ln1_gain, ln1_bias, ln2_gain, ln2_bias, b_out, b_fc2, jnp.zeros_like(b_out), jnp.zeros_like(b_out)]
    )
    vec_part = lax.dynamic_update_slice(
        jnp.zeros((8, width), f32), stacked, (0, row_at * feature_part)
    )
    inputs_own = own_frames(frames)
    cotangent_part = own_frames(cotangent)
    cotangent_all = lax.all_gather(cotangent_part, "col", axis=0, tiled=True)
    mask = jnp.concatenate([part_mask((part_at - shift) % parts) for shift in range(parts)])[None]
    block = pltpu.VMEM((slot, width), bf16)
    total = pltpu.VMEM((slot, width), f32)
    blocks = pltpu.VMEM((col_count - 1, slot, width), bf16)
    (
        vectors, wq, wkv, wo, normed_all, query_part, pair_whole, attended, log_total, residual,
        normed_two,
    ) = call(
        functools.partial(front_kernel, row_count, col_count), "front", 1, 4 * 10**10,
        [
            ((8, width), f32), ((width, head_width), bf16), ((width, 2 * head_width), bf16),
            ((width, head_width), bf16), ((held, width), bf16), ((held, head_width), bf16),
            ((parts * held, 2 * head_width), bf16), ((held, head_width), bf16),
            ((held, head_width // HEAD), f32), ((slot, width), f32), ((slot, width), bf16),
        ],
        [
            pltpu.VMEM((row_count - 1, 8, width), f32),
            pltpu.VMEM((width, head_width), bf16),
            pltpu.VMEM((width, 2 * head_width), bf16),
            pltpu.VMEM((width, head_width), bf16),
            block,
            pltpu.VMEM((held, width), bf16),
            pltpu.VMEM((held, 2 * head_width), bf16),
            pltpu.VMEM((held, 2 * head_width), bf16),
            blocks, blocks, total,
            dma((6, away)), dma((6, away)), dma((col_count,)), dma((col_count,)),
        ],
        inputs_own, vec_part, w_query, jnp.concatenate([w_key, w_value], axis=1), w_out.T,
        bias_query[None], bias_pair[None], mask,
    )
    block_part, d_branch_all, d_residual, grad_first, grad_second, small_two, hidden_sums = call(
        functools.partial(middle_kernel, col_count), "middle", 2, 4 * 10**10,
        [
            ((slot, width), bf16), ((held, width), bf16), ((slot, width), f32),
            ((width, hidden_part), bf16), ((width, hidden_part), bf16), ((4, width), f32),
            ((1, hidden_part), f32),
        ],
        [
            pltpu.VMEM((held, width), bf16),
            pltpu.VMEM((held, hidden_part), bf16),
            pltpu.VMEM((held, hidden_part), bf16),
            block,
            pltpu.VMEM((held, width), bf16),
            blocks, blocks, total, blocks, blocks, total,
            dma((4, away)), dma((4, away)),
        ],
        normed_two, residual, cotangent_part, cotangent_all, late[:, :hidden_part],
        late[:, hidden_part:], vectors, bias_hidden[None],
    )
    grad_part, small_one, query_sums, pair_sums, grad_q, grad_kv, grad_o = call(
        functools.partial(back_kernel, col_count), "back", 3, 4 * 10**10,
        [
            ((slot, width), bf16), ((2, width), f32), ((1, head_width), f32),
            ((1, 2 * head_width), f32), ((width, head_width), bf16),
            ((width, 2 * head_width), bf16), ((width, head_width), bf16),
        ],
        [
            pltpu.VMEM((held, head_width), bf16),
            pltpu.VMEM((parts * held, head_width), f32),
            pltpu.VMEM((parts * held, head_width), f32),
            pltpu.VMEM((2, held, head_width), bf16),
            pltpu.VMEM((2, held, head_width), bf16),
            pltpu.VMEM((held, 2 * head_width), bf16),
            blocks, blocks, total,
            dma((1, away)), dma((1, away)), dma((1,)), dma((1,)),
        ],
        inputs_own, d_residual, vectors, wq, wkv, wo, normed_all, query_part, pair_whole, attended,
        log_total, mask, d_branch_all,
    )
    joint_end = 3 * head_width
    late_grads = all_clips(reduce_rows(jnp.concatenate([grad_first, grad_second], axis=1)))
    early_grads = all_clips(reduce_rows(jnp.concatenate([grad_q, grad_kv, grad_o], axis=1)))
    featured = jnp.concatenate([small_one, small_two], axis=0).reshape(-1)
    headed = jnp.concatenate([query_sums[0], pair_sums[0, head_width:], hidden_sums[0]])
    sums = lax.psum(
        jnp.concatenate([featured, place_piece(headed, col_at, col_count)]), ("dp", "row", "col")
    )
    featured_sums = take_piece(
        sums[: 6 * width].reshape(6, row_count, feature_part).transpose(1, 0, 2), row_at, 1
    )[0]
    headed_sums = take_piece(sums[6 * width :], col_at, headed.shape[0])

    def whole_frames(piece):
        whole = lax.all_gather(piece, "row", axis=0, tiled=True)
        return whole.reshape(clip_count, parts * slot, width)[:, :frame_count]

    return (
        whole_frames(block_part),
        whole_frames(grad_part),
        featured_sums[0],
        featured_sums[1],
        early_grads[:, :head_width],
        headed_sums[:head_width],
        early_grads[:, head_width : 2 * head_width],
        early_grads[:, 2 * head_width : joint_end],
        headed_sums[head_width : 2 * head_width],
        early_grads[:, joint_end:].T,
        featured_sums[4],
        featured_sums[2],
        featured_sums[3],
        late_grads[:, :hidden_part],
        headed_sums[2 * head_width :],
        late_grads[:, hidden_part:],
        featured_sums[5],
    )


def solution(mesh):
    placed = (
        P("dp", "col", None),
        P("row"),
        P("row"),
        P("row", "col"),
        P(),
        P("row", "col"),
        P("row", "col"),
        P(),
        P("col", "row"),
        P("row"),
        P("row"),
        P("row"),
        P("row", "col"),
        P(),
        P("row", "col"),
        P("row"),
        P("dp", "col", None),
    )
    return jax.shard_map(
        local,
        mesh=mesh,
        in_specs=placed,
        out_specs=(
            P("dp", "col", None),
            P("dp", "col", None),
            P("row"),
            P("row"),
            P("row", "col"),
            P("col"),
            P("row", "col"),
            P("row", "col"),
            P("col"),
            P("col", "row"),
            P("row"),
            P("row"),
            P("row"),
            P("row", "col"),
            P("col"),
            P("row", "col"),
            P("row"),
        ),
        check_vma=False,
    )
```

time: 493 us -> 429 us (0.87)
  waiting for transfers between devices: 315 us -> 91.9 us
  Pallas kernels: 23.5 us -> 245 us
  matrix products: 37.2 us -> 0 us
  other arithmetic: 21.3 us -> 6.41 us
  blocking collectives: 46 us -> 40 us
    pallas_call x2 -> x3, Pallas kernels: 23.5 us -> 245 us  [call(): pl.pallas_call(kernel, in_specs=[pl.BlockSpec(memory_space=pltpu.VMEM)] *...]
    all_gather x4 -> x1, waiting for transfers between devices: 103 us -> 0.01 us  [local(): cotangent_all = lax.all_gather(cotangent_part, 'col', axis=0, tiled=True)]
    unnamed x17 -> x7, waiting for transfers between devices: 49.9 us -> 1.14 us
    reduce_scatter x4 -> x2, waiting for transfers between devices: 110 us -> 62.2 us  [reduce_rows(): lax.psum_scatter(tensor.astype(jnp.bfloat16), 'row', scatter_dimension=0,...]
    dot_general x12 -> x0, matrix products: 37.2 us -> none  [mix(): lax.dot_general(first, second, (((first_dim,), (second_dim,)), ((), ())),...]
    all_gather x2 -> x1, waiting for transfers between devices: 36.1 us -> 0.02 us  [gather_rows(): return lax.all_gather(tensor, 'row', axis=0, tiled=True)]
    psum x1, waiting for transfers between devices: 0.82 us -> 28.5 us  [all_clips(): return lax.psum(tensor.astype(jnp.bfloat16), 'dp').astype(jnp.float32)]
    all_gather x2, waiting for transfers between devices: 12.4 us -> 0.01 us  [whole_frames(): whole = lax.all_gather(piece, 'row', axis=0, tiled=True)]
  transfers between devices with their start and end apart: 17 -> 7, of which waited for: 16 -> 3; matrix products, arithmetic and copies ran while one was open for 14% -> 4% of each run, Pallas kernels for 3% -> 18%
where the time goes in v2:
time: 429 us; the launch traced here: 428 us
  Pallas kernels  245 us (57%)
  waiting for transfers between devices  91.9 us (21%)
  blocking collectives  40 us (9%)
  local copies, waits for them, and re-layouts  29.4 us (7%)
  between operations  14.6 us (3%)
  other arithmetic  6.41 us (1%)
    pallas_call x3, Pallas kernels, call(): pl.pallas_call(kernel, in_specs=[pl.BlockSpec(memory_space=pltpu.VMEM)] *...  245 us
    reduce_scatter x2, waiting for transfers between devices, reduce_rows(): lax.psum_scatter(tensor.astype(jnp.bfloat16), 'row', scatter_dimension=0,...  62.2 us
    psum x1, blocking collectives, local(): lax.psum(jnp.concatenate([featured, place_piece(headed, col_at, col_count...  40 us
    psum x1, waiting for transfers between devices, all_clips(): return lax.psum(tensor.astype(jnp.bfloat16), 'dp').astype(jnp.float32)  28.5 us
    unnamed x66, local copies, waits for them, and re-layouts  14.9 us
  transfers between devices with their start and end apart: 7, of which 3 were waited for; matrix products, arithmetic and copies ran while one was open for 4% of the time, Pallas kernels for 18%

profile of v2, /device:TPU:0, one launch (start us, length us, event | category | flops | bytes accessed | tf_op | source)
XLA Modules:
  0.0 428.0 jit_solution(8275101280434464003)
XLA Ops:
  7.2 0.0 all-gather.6.cloned.1.call-start
  7.2 2.0 pad_maximum_fusion.2
  9.3 0.0 all-gather.12.cloned.1.call-start
  9.3 0.1 copy.41
  9.5 0.8 pad_dynamic-slice_fusion
  10.3 0.0 all-gather.12.cloned.1.call-update
  10.3 0.0 reduce-scatter.3.cloned.1.call-start
  10.4 0.5 copy-done.20
  10.8 0.1 copy.39
  11.1 0.1 fusion.x_ref
  11.2 0.1 tile.21
  11.3 0.1 tile.9
  11.4 0.8 dynamic_slice.23
  12.2 0.1 concatenate.28
  12.2 0.8 dynamic_slice.22
  13.0 0.1 copy.40
  13.1 0.1 pad_maximum_fusion.3.wkv_ref
  13.3 0.3 dynamic_update_slice.6.vec_ref
  13.6 77.6 %front.1 = (f32[8,768]{1,0:T(8,128)S(1)}, bf16[768,192]{1,0:T(8,128)(2,1)S(1)}, bf16[768,384]{1,0:T(8,128)(2,1)S(1)}, bf16[768,192]{1,0:T(8,128)(2,1)S(1)}, bf16...) custom-call(bf16[192,768]{1,0:T(8,128)(2,1)S(1)} %fusion.x_ref, ...), custom_call_target="tpu_custom_call" | custom-call | flops 40000000000 | bytes 60000000 | tf_op jit(solution)/shard_map/front/pallas_call | solution.py:479
  91.3 1.0 copy-done.1
  92.3 0.8 copy-done.3
  93.1 0.8 copy-done.5
  93.9 0.7 copy-done.7
  94.7 0.8 copy-done.9
  95.5 0.7 copy-done.11
  96.2 0.8 copy-done.13
  97.0 0.7 copy-done.15
  97.7 0.8 dynamic_slice.25
  98.5 0.1 fusion.7.cot_ref
  98.6 0.0 all-gather.6.cloned.1.call-done
  98.6 3.3 fusion.1
  101.8 1.1 copy-done.6
  102.9 1.0 copy-done.16
  103.9 122.0 %middle.1 = (bf16[192,768]{1,0:T(8,128)(2,1)}, bf16[768,768]{1,0:T(8,128)(2,1)S(1)}, f32[192,768]{1,0:T(8,128)S(1)}, bf16[768,768]{1,0:T(8,128)(2,1)S(1)}, bf16[...) custom-call(bf16[192,768]{1,0:T(8,128)(2,1)S(1)} %copy-done.16, f32[192,768]{1,0:T(8,128)S(1)} %copy-done.6, ...), custom_call_target="tpu_custom_call" | custom-call | flops 40000000000 | bytes 60000000 | tf_op jit(solution)/shard_map/middle/pallas_call | solution.py:479
  225.9 1.0 copy-done.2
  227.0 45.7 %back.1 = (bf16[192,768]{1,0:T(8,128)(2,1)}, f32[2,768]{1,0:T(2,128)S(1)}, f32[1,192]{1,0:T(1,128)S(1)}, f32[1,384]{1,0:T(1,128)S(1)}, bf16[768,192]{1,0:T(8,128...) custom-call(bf16[192,768]{1,0:T(8,128)(2,1)S(1)} %fusion.x_ref, ...), custom_call_target="tpu_custom_call" | custom-call | flops 40000000000 | bytes 60000000 | tf_op jit(solution)/shard_map/back/pallas_call | solution.py:479
  272.7 1.6 pad_maximum_fusion.1
  274.3 0.0 reduce-scatter.5.cloned.1.call-start
  274.4 1.6 pad_maximum_fusion
  276.0 0.0 all-gather.10.cloned.1.call-start
  276.1 0.5 all-gather.10.cloned.1.call-update
  276.6 0.0 all-gather.8.cloned.1.call-start
  276.7 0.5 all-gather.8.cloned.1.call-update
  277.2 0.0 all-reduce.6.cloned.1.call-start
  277.3 0.1 slice.84
  277.4 0.1 concatenate.32
  277.4 0.3 dynamic_update_slice.7
  277.7 26.5 %reduce-scatter.3.cloned.1.call-done = bf16[192,768]{1,0:T(8,128)(2,1)} async-done(((bf16[768,768]{1,0:T(8,128)(2,1)}), bf16[192,768]{1,0:T(8,128)(2,1)}) %reduce-scatter.3.cloned.1.call-update) | async-done | bytes 294928 | tf_op jit(solution)/shard_map/reduce_scatter | solution.py:27
  304.2 35.7 %reduce-scatter.5.cloned.1.call-done = bf16[192,1536]{1,0:T(8,128)(2,1)} async-done(((bf16[768,1536]{1,0:T(8,128)(2,1)}), bf16[192,1536]{1,0:T(8,128)(2,1)}) %reduce-scatter.5.cloned.1.call-update) | async-done | bytes 589840 | tf_op jit(solution)/shard_map/reduce_scatter | solution.py:27
  339.9 40.0 %psum.21 = f32[9216]{0:T(1024)S(1)} all-reduce(f32[9216]{0:T(1024)S(1)} %pad_maximum_fusion.4), channel_id=1, replica_groups=mesh['dp'=2,'row'=4,'col'=4] {'dp','row','col'}, use_global_device_ids=true, to_apply=%region_0.1 | all-reduce | flops 9216 | bytes 73728 | tf_op jit(solution)/shard_map/psum | solution.py:628
  379.9 0.1 reshape.82
  380.0 0.7 dynamic-slice.6
  380.7 0.6 fusion.5
  381.4 0.6 fusion.6
  381.9 1.3 slice.105
  383.3 1.9 copy.46
  385.2 1.5 slice.104
  386.7 1.9 copy.45
  388.6 28.5 %all-reduce.6.cloned.1.call-done = (bf16[192,1536]{1,0:T(8,128)(2,1)}, bf16[192,768]{1,0:T(8,128)(2,1)}) async-done(((bf16[192,1536]{1,0:T(8,128)(2,1)}, bf16[192,768]{1,0:T(8,128)(2,1)}), (bf16[192,1536]{1,0:T(8,128)(2,1)}, bf16[192,768]{1,0:T(8,128)(2,1)})) %all-reduce.6.cloned.1.call-update) | async-done | bytes 884752 | tf_op jit(solution)/shard_map/psum | solution.py:33
  417.2 1.1 convert_element_type.7
  418.3 0.8 fusion.3
  419.1 1.1 fusion.2
  420.2 0.1 slice_bitcast_fusion
  420.3 0.8 copy.44
  (73 shorter events, 0.3 us)
Async XLA Ops:
  7.2 2.2 copy-start.19
  7.2 91.4 %all-gather.6.cloned.1.call-start = ((), (), s32[]{:S(2)}) async-start(), calls=%async_computation.2 | async-start | bytes 2949120 | tf_op jit(solution)/shard_map/all_gather | solution.py:23
  9.3 92.6 %all-gather.12.cloned.1.call-start = ((), (), s32[]{:S(2)}) async-start(), calls=%async_computation.7 | async-start | bytes 1474560 | tf_op jit(solution)/shard_map/all_gather | solution.py:553
  9.5 1.4 copy-start.20
  10.3 293.9 %reduce-scatter.3.cloned.1.call-start = ((), (), s32[]{:S(2)}) async-start(), calls=%async_computation.5 | async-start | bytes 1474560 | tf_op jit(solution)/shard_map/reduce_scatter | solution.py:27
  11.0 2.0 copy-start.21
  11.0 2.1 copy-start.22
  11.0 2.1 copy-start.23
  11.0 2.2 copy-start.24
  11.0 2.2 copy-start.25
  11.0 2.2 copy-start.26
  11.0 2.2 copy-start.27
  11.1 2.2 copy-start.28
  11.1 2.2 copy-start.29
  11.1 2.6 copy-start
  91.3 1.0 copy-start.1
  92.3 0.8 copy-start.3
  93.1 0.8 copy-start.5
  93.9 0.7 copy-start.7
  94.7 0.8 copy-start.9
  95.5 0.7 copy-start.11
  96.2 0.8 copy-start.13
  97.0 0.7 copy-start.15
  101.8 1.1 copy-start.6
  102.9 1.0 copy-start.16
  103.9 123.1 %copy-start.4 = (bf16[768,384]{1,0:T(8,128)(2,1)S(1)}, bf16[768,384]{1,0:T(8,128)(2,1)}, u32[]{:S(2)}) copy-start(bf16[768,384]{1,0:T(8,128)(2,1)} %copy-done.3) | copy-start | bytes 1769476
  103.9 123.1 %copy-start.8 = (bf16[768,192]{1,0:T(8,128)(2,1)S(1)}, bf16[768,192]{1,0:T(8,128)(2,1)}, u32[]{:S(2)}) copy-start(bf16[768,192]{1,0:T(8,128)(2,1)} %copy-done.7) | copy-start | bytes 884740
  103.9 123.1 %copy-start.10 = (bf16[768,192]{1,0:T(8,128)(2,1)S(1)}, bf16[768,192]{1,0:T(8,128)(2,1)}, u32[]{:S(2)}) copy-start(bf16[768,192]{1,0:T(8,128)(2,1)} %copy-done.9) | copy-start | bytes 884740
  103.9 123.1 %copy-start.12 = (bf16[768,192]{1,0:T(8,128)(2,1)S(1)}, bf16[768,192]{1,0:T(8,128)(2,1)}, u32[]{:S(2)}) copy-start(bf16[768,192]{1,0:T(8,128)(2,1)} %copy-done.11) | copy-start | bytes 884740
  103.9 123.1 %copy-start.14 = (f32[768,3]{1,0:T(8,128)S(1)}, f32[768,3]{1,0:T(8,128)}, u32[]{:S(2)}) copy-start(f32[768,3]{1,0:T(8,128)} %copy-done.13) | copy-start | bytes 27652
  225.9 1.0 copy-start.2
  274.3 65.6 %reduce-scatter.5.cloned.1.call-start = ((), (), s32[]{:S(2)}) async-start(), calls=%async_computation.6 | async-start | bytes 2949120 | tf_op jit(solution)/shard_map/reduce_scatter | solution.py:27
  276.0 105.9 %all-gather.10.cloned.1.call-start = ((), (), s32[]{:S(2)}) async-start(), calls=%async_computation.4 | async-start | bytes 1474560 | tf_op jit(solution)/shard_map/all_gather | solution.py:637
  276.6 108.6 %all-gather.8.cloned.1.call-start = ((), (), s32[]{:S(2)}) async-start(), calls=%async_computation.3 | async-start | bytes 1474560 | tf_op jit(solution)/shard_map/all_gather | solution.py:637
  277.2 140.0 %all-reduce.6.cloned.1.call-start = ((), (), s32[]{:S(2)}) async-start(), calls=%async_computation.8 | async-start | bytes 1769472 | tf_op jit(solution)/shard_map/psum | solution.py:33
  417.2 1.1 copy-start.17
  417.2 1.9 copy-start.18
Sparse Core Ops, SparseCore 0:
  10.2 39.3 all-gather.5
  51.1 47.2 all-gather.11
  274.5 29.7 reduce-scatter.2
  306.8 33.0 reduce-scatter.4
  341.3 17.6 all-gather.9
  360.4 17.5 all-gather.7
  380.3 36.8 all-reduce.5

commit v3 on v2

--- a/solution.py
+++ b/solution.py
@@ -7,7 +7,7 @@
 from jax.sharding import PartitionSpec as P
 
 HEAD = 64
-VMEM_LIMIT = 48 * 1024 * 1024
+VMEM_LIMIT = 56 * 1024 * 1024
 
 
 def mix(first, second, first_dim, second_dim):
@@ -21,22 +21,6 @@
 
 def gather_rows(tensor):
     return lax.all_gather(tensor, "row", axis=0, tiled=True)
-
-
-def reduce_rows(tensor):
-    return lax.psum_scatter(
-        tensor.astype(jnp.bfloat16), "row", scatter_dimension=0, tiled=True
-    ).astype(jnp.float32)
-
-
-def all_clips(tensor):
-    return lax.psum(tensor.astype(jnp.bfloat16), "dp").astype(jnp.float32)
-
-
-def place_piece(vector, piece_index, piece_count):
-    piece_size = vector.shape[0]
-    filled = jnp.zeros((piece_size * piece_count,), jnp.float32)
-    return lax.dynamic_update_slice(filled, vector, (piece_index * piece_size,))
 
 
 def take_piece(vector, piece_index, piece_size):
@@ -95,6 +79,54 @@
             self.copy(step).wait_send()
 
 
+class Scatter:
+    def __init__(self, axis, count, source, incoming, sends, recvs, row):
+        self.axis, self.count, self.me = axis, count, lax.axis_index(axis)
+        self.source, self.incoming, self.row = source, incoming, row
+        self.sends, self.recvs = sends, recvs
+
+    def copy(self, step):
+        peer = ring(self.me, step, self.count)
+        return put(
+            self.source.at[span(peer, self.incoming.shape[1])],
+            self.incoming.at[step - 1],
+            self.sends.at[self.row, step - 1],
+            self.recvs.at[self.row, step - 1],
+            self.axis,
+            peer,
+        )
+
+    def start(self):
+        for step in range(1, self.count):
+            self.copy(step).start()
+
+    def total(self):
+        own = self.source[span(self.me, self.incoming.shape[1]), :].astype(jnp.float32)
+        for step in range(1, self.count):
+            self.copy(step).wait_recv()
+            own = own + self.incoming[step - 1].astype(jnp.float32)
+        return own
+
+    def finish(self):
+        for step in range(1, self.count):
+            self.copy(step).wait_send()
+
+
+class Share(Gather):
+    def begin(self, value):
+        self.source[...] = value.astype(self.source.dtype)
+        self.start()
+        self.keep_own()
+
+    def total(self):
+        size = self.source.shape[0]
+        self.wait()
+        result = self.whole[0:size, :].astype(jnp.float32)
+        for at in range(1, self.count):
+            result = result + self.whole[at * size : (at + 1) * size, :].astype(jnp.float32)
+        return result
+
+
 class Reduce:
     def __init__(self, axis, count, outgoing, incoming, sends, recvs, row, toward=1):
         self.axis, self.count, self.me = axis, count, lax.axis_index(axis)
@@ -166,10 +198,10 @@
 
 def front_kernel(
     n_row, n_col,
-    x_ref, vec_ref, wq_ref, wkv_ref, wo_ref, bq_ref, bkv_ref, mask_ref,
+    x_ref, cot_ref, vec_ref, wq_ref, wkv_ref, wo_ref, bq_ref, bkv_ref, mask_ref,
     vec_out, wq_out, wkv_out, wo_out, normed_out, query_out, pair_out, att_out, total_out,
-    resid_out, normed2_out,
-    vec_buf, wq_buf, wkv_buf, wo_buf, own_buf, normed_buf, pair_buf, away_buf, sum_out, sum_in,
+    resid_out, normed2_out, cot_out,
+    cot_buf, vec_buf, wq_buf, wkv_buf, wo_buf, own_buf, normed_buf, pair_buf, away_buf, sum_out, sum_in,
     own_sum, sends, recvs, pair_sends, pair_recvs,
 ):
     slot = x_ref.shape[0]
@@ -237,6 +269,9 @@
         return carry
 
     lax.fori_loop(0, n_col, project, 0)
+    cots = Gather("col", n_col, cot_ref, cot_buf, sends, recvs, 6)
+    cots.start()
+    cots.keep_own()
     for at in range(n_col):
         pair_copy(at).wait_recv()
     pair_out[0:held, :] = pair_buf[...]
@@ -283,6 +318,9 @@
     resid_out[...] = residual
     scaled, _ = norm_stats(residual)
     normed2_out[...] = (scaled * vectors[2:3] + vectors[3:4]).astype(jnp.bfloat16)
+    cots.wait()
+    cot_out[...] = cot_buf[...]
+    cots.finish()
     for copy in vec_copies:
         copy.wait_send()
     for gather in gathers:
@@ -296,9 +334,8 @@
 def middle_kernel(
     n_col,
     normed2_ref, resid_ref, cot_ref, cot_all_ref, w1_ref, w2_ref, vec_ref, bh_ref,
-    block_out, d_branch_out, d_resid_out, g1_out, g2_out, small_out, hidden_sum_out,
-    normed_buf, hidden_buf, d_pre_buf, d_own, d_buf, sum_out, sum_in, own_sum, last_out, last_in,
-    own_last, sends, recvs,
+    hidden_out, d_branch_out, d_resid_out, g1_out, g2_out, small_out, hidden_sum_out,
+    normed_buf, d_pre_buf, d_own, d_buf, sum_out, sum_in, own_sum, sends, recvs,
 ):
     slot = resid_ref.shape[0]
     col_at = lax.axis_index("col")
@@ -307,7 +344,6 @@
     frames.start()
     frames.keep_own()
     sums = Reduce("col", n_col, sum_out, sum_in, sends, recvs, 1, -1)
-    lasts = Reduce("col", n_col, last_out, last_in, sends, recvs, 2, -1)
 
     def feed(step, carry):
         sender = ring(col_at, n_col - step, n_col)
@@ -320,7 +356,7 @@
         pre = mix(block, w1_ref[...], 1, 0) + bh_ref[...]
         normal = 0.5 * (1.0 + lax.erf(pre * 0.7071067811865476))
         hidden = (pre * normal).astype(jnp.bfloat16)
-        hidden_buf[span(sender, slot), :] = hidden
+        hidden_out[span(sender, slot), :] = hidden
         slope = normal + pre * (0.3989422804014327 * jnp.exp(-0.5 * pre * pre))
         terms = mix(cot_all_ref[span(sender, slot), :], w2_ref[...], 1, 0)
         d_pre = (terms * slope).astype(jnp.bfloat16)
@@ -348,23 +384,8 @@
     backs = Gather("col", n_col, d_own, d_buf, sends, recvs, 3)
     backs.start()
     backs.keep_own()
-    def finish_block(step, carry):
-        sender = ring(col_at, n_col - step, n_col)
-        partial = mix(hidden_buf[span(sender, slot), :], w2_ref[...], 1, 1)
-
-        @pl.when(step > 0)
-        def _():
-            lasts.send(step, partial)
-
-        @pl.when(step == 0)
-        def _():
-            own_last[...] = partial
-
-        return carry
-
-    lax.fori_loop(0, n_col, finish_block, 0)
     g1_out[...] = mix(normed_buf[...], d_pre_buf[...], 0, 0).astype(jnp.bfloat16)
-    g2_out[...] = mix(cot_all_ref[...], hidden_buf[...], 0, 0).astype(jnp.bfloat16)
+    g2_out[...] = mix(cot_all_ref[...], hidden_out[...], 0, 0).astype(jnp.bfloat16)
     hidden_sum_out[...] = column_sums(d_pre_buf[...].astype(jnp.float32))
     small_out[...] = jnp.concatenate(
         [
@@ -377,29 +398,54 @@
     )
     backs.wait()
     d_branch_out[...] = d_buf[...]
-    block_out[...] = (
-        resid_ref[...] + lasts.total(own_last[...]) + vec_ref[5:6, :]
-    ).astype(jnp.bfloat16)
     frames.finish()
     sums.finish()
-    lasts.finish()
     backs.finish()
 
 
 def back_kernel(
-    n_col,
+    n_dp, n_row, n_col,
     x_ref, d_resid_ref, vec_ref, wq_ref, wkv_ref, wo_ref, normed_ref, query_ref, pair_ref,
-    att_ref, total_ref, mask_ref, d_branch_ref,
-    frames_out, small_out, bq_out, bkv_out, gq_out, gkv_out, go_out,
+    att_ref, total_ref, mask_ref, d_branch_ref, hidden_ref, w2_ref, resid_ref, g1_ref, g2_ref,
+    small_two_ref, hidden_sum_ref,
+    block_out, frames_out, feature_out, head_out, g1_out, g2_out, gq_out, gkv_out, go_out,
     d_query_buf, d_key_buf, d_value_buf, pair_buf, away_buf, d_pair_buf, sum_out, sum_in, own_sum,
+    last_out, last_in, own_last, own_block, block_buf, own_frames, frames_buf,
+    gq_buf, gkv_buf, go_buf, g1_in, g2_in, gq_in, gkv_in, go_in,
+    g1_own, g2_own, gq_own, gkv_own, go_own, g1_dp, g2_dp, gq_dp, gkv_dp, go_dp,
+    feature_own, feature_buf, small_own, small_buf, last_own, last_buf,
     sends, recvs, pair_sends, pair_recvs,
 ):
     slot = x_ref.shape[0]
     head_width = wq_ref.shape[1]
     held = slot * n_col
+    width = x_ref.shape[1]
     col_at = lax.axis_index("col")
     partner = partner_row()
-    greet([("row", partner)] + others("col", n_col))
+    greet(others("row", n_row) + others("col", n_col) + others("dp", n_dp))
+    late = [
+        Scatter("row", n_row, g1_ref, g1_in, sends, recvs, 2),
+        Scatter("row", n_row, g2_ref, g2_in, sends, recvs, 3),
+    ]
+    for scatter in late:
+        scatter.start()
+    lasts = Reduce("col", n_col, last_out, last_in, sends, recvs, 1, -1)
+
+    def finish_block(step, carry):
+        sender = ring(col_at, n_col - step, n_col)
+        partial = mix(hidden_ref[span(sender, slot), :], w2_ref[...], 1, 1)
+
+        @pl.when(step > 0)
+        def _():
+            lasts.send(step, partial)
+
+        @pl.when(step == 0)
+        def _():
+            own_last[...] = partial
+
+        return carry
+
+    lax.fori_loop(0, n_col, finish_block, 0)
     d_key_buf[...] = jnp.zeros_like(d_key_buf)
     d_value_buf[...] = jnp.zeros_like(d_value_buf)
     mask = mask_ref[...]
@@ -435,8 +481,8 @@
     pair_buf[1] = d_value_buf[held : 2 * held, :].astype(jnp.bfloat16)
     crossing = put(pair_buf, away_buf, pair_sends.at[0], pair_recvs.at[0], "row", partner)
     crossing.start()
-    gq_out[...] = mix(normed_ref[...], d_query_buf[...], 0, 0).astype(jnp.bfloat16)
-    go_out[...] = mix(d_branch_ref[...], att_ref[...], 0, 0).astype(jnp.bfloat16)
+    gq_buf[...] = mix(normed_ref[...], d_query_buf[...], 0, 0).astype(jnp.bfloat16)
+    go_buf[...] = mix(d_branch_ref[...], att_ref[...], 0, 0).astype(jnp.bfloat16)
     crossing.wait_recv()
     d_key = d_key_buf[0:held, :] + away_buf[0].astype(jnp.float32)
     d_value = d_value_buf[0:held, :] + away_buf[1].astype(jnp.float32)
@@ -460,19 +506,89 @@
         return carry
 
     lax.fori_loop(1, n_col + 1, spread, 0)
-    gkv_out[...] = mix(normed_ref[...], d_pair_buf[...], 0, 0).astype(jnp.bfloat16)
-    bq_out[...] = column_sums(d_query_buf[...].astype(jnp.float32))
-    bkv_out[...] = column_sums(d_pair_buf[...].astype(jnp.float32))
+    gkv_buf[...] = mix(normed_ref[...], d_pair_buf[...], 0, 0).astype(jnp.bfloat16)
+    early = [
+        Scatter("row", n_row, gq_buf, gq_in, sends, recvs, 6),
+        Scatter("row", n_row, gkv_buf, gkv_in, sends, recvs, 7),
+        Scatter("row", n_row, go_buf, go_in, sends, recvs, 8),
+    ]
+    for scatter in early:
+        scatter.start()
+    late_shares = [
+        Share("dp", n_dp, g1_own, g1_dp, sends, recvs, 9),
+        Share("dp", n_dp, g2_own, g2_dp, sends, recvs, 10),
+    ]
+    for scatter, share in zip(late, late_shares):
+        share.begin(scatter.total())
+    own_block[...] = (
+        resid_ref[...] + lasts.total(own_last[...]) + vec_ref[5:6, :]
+    ).astype(jnp.bfloat16)
+    blocks = Gather("row", n_row, own_block, block_buf, sends, recvs, 4)
+    blocks.start()
+    blocks.keep_own()
+    query_sums = column_sums(d_query_buf[...].astype(jnp.float32))
+    pair_sums = column_sums(d_pair_buf[...].astype(jnp.float32))
     scaled, inv_std = norm_stats(x_ref[...].astype(jnp.float32))
     d_normed = sums.total(own_sum[...])
-    frames_out[...] = (
+    own_frames[...] = (
         d_resid_ref[...] + norm_backward(d_normed, scaled, inv_std, vec_ref[0:1, :])
     ).astype(jnp.bfloat16)
-    small_out[...] = jnp.concatenate(
-        [column_sums(d_normed * scaled), column_sums(d_normed)], axis=0
-    )
+    wholes = Gather("row", n_row, own_frames, frames_buf, sends, recvs, 5)
+    wholes.start()
+    wholes.keep_own()
+    features = Share("col", n_col, feature_own, feature_buf, sends, recvs, 14)
+    features.begin(
+        jnp.concatenate(
+            [
+                column_sums(d_normed * scaled),
+                column_sums(d_normed),
+                small_two_ref[...],
+                jnp.zeros((2, width), jnp.float32),
+            ],
+            axis=0,
+        )
+    )
+    early_shares = [
+        Share("dp", n_dp, gq_own, gq_dp, sends, recvs, 11),
+        Share("dp", n_dp, gkv_own, gkv_dp, sends, recvs, 12),
+        Share("dp", n_dp, go_own, go_dp, sends, recvs, 13),
+    ]
+    for scatter, share in zip(early, early_shares):
+        share.begin(scatter.total())
+    heads = jnp.concatenate(
+        [query_sums, pair_sums, jnp.zeros((1, width - 3 * head_width), jnp.float32)], axis=1
+    )
+    smalls = Share("row", n_row, small_own, small_buf, sends, recvs, 15)
+    smalls.begin(
+        jnp.concatenate(
+            [
+                features.total(),
+                hidden_sum_ref[...],
+                heads,
+                jnp.zeros((6, width), jnp.float32),
+            ],
+            axis=0,
+        )
+    )
+    finals = Share("dp", n_dp, last_own, last_buf, sends, recvs, 16)
+    finals.begin(smalls.total())
+    g1_out[...] = late_shares[0].total()
+    g2_out[...] = late_shares[1].total()
+    gq_out[...] = early_shares[0].total()
+    gkv_out[...] = early_shares[1].total()
+    go_out[...] = early_shares[2].total()
+    blocks.wait()
+    block_out[...] = block_buf[...]
+    wholes.wait()
+    frames_out[...] = frames_buf[...]
+    summed = finals.total()
+    feature_out[...] = summed[0:8]
+    head_out[...] = summed[8:16]
     crossing.wait_send()
-    sums.finish()
+    for sent in [sums, lasts, blocks, wholes, features, smalls, finals]:
+        sent.finish()
+    for sent in late + early + late_shares + early_shares:
+        sent.finish()
 
 
 def call(kernel, name, number, flops, outs, scratch, *operands):
@@ -535,7 +651,7 @@
 
     bf16, f32 = jnp.bfloat16, jnp.float32
     held = slot * col_count
-    away = max(row_count, col_count) - 1
+    away = max(row_count, col_count, lax.axis_size("dp")) - 1
     dma = pltpu.SemaphoreType.DMA
     late = gather_rows(jnp.concatenate([w_fc1, w_fc2], axis=1))
     bias_query = take_piece(b_query, col_at, head_width)
@@ -550,14 +666,14 @@
     )
     inputs_own = own_frames(frames)
     cotangent_part = own_frames(cotangent)
-    cotangent_all = lax.all_gather(cotangent_part, "col", axis=0, tiled=True)
+    dp_count = lax.axis_size("dp")
     mask = jnp.concatenate([part_mask((part_at - shift) % parts) for shift in range(parts)])[None]
     block = pltpu.VMEM((slot, width), bf16)
     total = pltpu.VMEM((slot, width), f32)
     blocks = pltpu.VMEM((col_count - 1, slot, width), bf16)
     (
         vectors, wq, wkv, wo, normed_all, query_part, pair_whole, attended, log_total, residual,
-        normed_two,
+        normed_two, cotangent_all,
     ) = call(
         functools.partial(front_kernel, row_count, col_count), "front", 1, 4 * 10**10,
         [
@@ -565,8 +681,10 @@
             ((width, head_width), bf16), ((held, width), bf16), ((held, head_width), bf16),
             ((parts * held, 2 * head_width), bf16), ((held, head_width), bf16),
             ((held, head_width // HEAD), f32), ((slot, width), f32), ((slot, width), bf16),
+            ((held, width), bf16),
         ],
         [
+            pltpu.VMEM((held, width), bf16),
             pltpu.VMEM((row_count - 1, 8, width), f32),
             pltpu.VMEM((width, head_width), bf16),
             pltpu.VMEM((width, 2 * head_width), bf16),
@@ -576,36 +694,45 @@
             pltpu.VMEM((held, 2 * head_width), bf16),
             pltpu.VMEM((held, 2 * head_width), bf16),
             blocks, blocks, total,
-            dma((6, away)), dma((6, away)), dma((col_count,)), dma((col_count,)),
+            dma((7, away)), dma((7, away)), dma((col_count,)), dma((col_count,)),
         ],
-        inputs_own, vec_part, w_query, jnp.concatenate([w_key, w_value], axis=1), w_out.T,
+        inputs_own, cotangent_part, vec_part, w_query, jnp.concatenate([w_key, w_value], axis=1), w_out.T,
         bias_query[None], bias_pair[None], mask,
     )
-    block_part, d_branch_all, d_residual, grad_first, grad_second, small_two, hidden_sums = call(
+    hidden_all, d_branch_all, d_residual, grad_first, grad_second, small_two, hidden_sums = call(
         functools.partial(middle_kernel, col_count), "middle", 2, 4 * 10**10,
         [
-            ((slot, width), bf16), ((held, width), bf16), ((slot, width), f32),
+            ((held, hidden_part), bf16), ((held, width), bf16), ((slot, width), f32),
             ((width, hidden_part), bf16), ((width, hidden_part), bf16), ((4, width), f32),
             ((1, hidden_part), f32),
         ],
         [
             pltpu.VMEM((held, width), bf16),
             pltpu.VMEM((held, hidden_part), bf16),
-            pltpu.VMEM((held, hidden_part), bf16),
             block,
             pltpu.VMEM((held, width), bf16),
-            blocks, blocks, total, blocks, blocks, total,
+            blocks, blocks, total,
             dma((4, away)), dma((4, away)),
         ],
         normed_two, residual, cotangent_part, cotangent_all, late[:, :hidden_part],
         late[:, hidden_part:], vectors, bias_hidden[None],
     )
-    grad_part, small_one, query_sums, pair_sums, grad_q, grad_kv, grad_o = call(
-        functools.partial(back_kernel, col_count), "back", 3, 4 * 10**10,
+    head = (feature_part, head_width)
+    pair = (feature_part, 2 * head_width)
+    hide = (feature_part, hidden_part)
+
+    def several(count, *shapes):
+        return [pltpu.VMEM((count,) + shape, bf16) for shape in shapes]
+
+    def stacks(count, *shapes):
+        return [pltpu.VMEM((count * shape[0], shape[1]), bf16) for shape in shapes]
+
+    block_all, grad_all, features, heads, grad_1, grad_2, grad_q, grad_kv, grad_o = call(
+        functools.partial(back_kernel, dp_count, row_count, col_count), "back", 3, 4 * 10**10,
         [
-            ((slot, width), bf16), ((2, width), f32), ((1, head_width), f32),
-            ((1, 2 * head_width), f32), ((width, head_width), bf16),
-            ((width, 2 * head_width), bf16), ((width, head_width), bf16),
+            ((row_count * slot, width), bf16), ((row_count * slot, width), bf16),
+            ((8, width), f32), ((8, width), f32),
+            (hide, f32), (hide, f32), (head, f32), (pair, f32), (head, f32),
         ],
         [
             pltpu.VMEM((held, head_width), bf16),
@@ -614,46 +741,48 @@
             pltpu.VMEM((2, held, head_width), bf16),
             pltpu.VMEM((2, held, head_width), bf16),
             pltpu.VMEM((held, 2 * head_width), bf16),
-            blocks, blocks, total,
-            dma((1, away)), dma((1, away)), dma((1,)), dma((1,)),
+            blocks, blocks, total, blocks, blocks, total,
+            block, pltpu.VMEM((row_count * slot, width), bf16),
+            block, pltpu.VMEM((row_count * slot, width), bf16),
+        ]
+        + stacks(row_count, head, pair, head)
+        + several(row_count - 1, hide, hide, head, pair, head)
+        + stacks(1, hide, hide, head, pair, head)
+        + stacks(dp_count, hide, hide, head, pair, head)
+        + [
+            pltpu.VMEM((8, width), f32), pltpu.VMEM((col_count * 8, width), f32),
+            pltpu.VMEM((16, width), f32), pltpu.VMEM((row_count * 16, width), f32),
+            pltpu.VMEM((16, width), f32), pltpu.VMEM((dp_count * 16, width), f32),
+            dma((17, away)), dma((17, away)), dma((1,)), dma((1,)),
         ],
         inputs_own, d_residual, vectors, wq, wkv, wo, normed_all, query_part, pair_whole, attended,
-        log_total, mask, d_branch_all,
-    )
-    joint_end = 3 * head_width
-    late_grads = all_clips(reduce_rows(jnp.concatenate([grad_first, grad_second], axis=1)))
-    early_grads = all_clips(reduce_rows(jnp.concatenate([grad_q, grad_kv, grad_o], axis=1)))
-    featured = jnp.concatenate([small_one, small_two], axis=0).reshape(-1)
-    headed = jnp.concatenate([query_sums[0], pair_sums[0, head_width:], hidden_sums[0]])
-    sums = lax.psum(
-        jnp.concatenate([featured, place_piece(headed, col_at, col_count)]), ("dp", "row", "col")
-    )
-    featured_sums = take_piece(
-        sums[: 6 * width].reshape(6, row_count, feature_part).transpose(1, 0, 2), row_at, 1
-    )[0]
-    headed_sums = take_piece(sums[6 * width :], col_at, headed.shape[0])
-
-    def whole_frames(piece):
-        whole = lax.all_gather(piece, "row", axis=0, tiled=True)
+        log_total, mask, d_branch_all, hidden_all, late[:, hidden_part:], residual, grad_first,
+        grad_second, small_two, hidden_sums,
+    )
+    featured_sums = lax.dynamic_slice(
+        features, (0, row_at * feature_part), (features.shape[0], feature_part)
+    )
+
+    def whole_frames(whole):
         return whole.reshape(clip_count, parts * slot, width)[:, :frame_count]
 
     return (
-        whole_frames(block_part),
-        whole_frames(grad_part),
+        whole_frames(block_all),
+        whole_frames(grad_all),
         featured_sums[0],
         featured_sums[1],
-        early_grads[:, :head_width],
-        headed_sums[:head_width],
-        early_grads[:, head_width : 2 * head_width],
-        early_grads[:, 2 * head_width : joint_end],
-        headed_sums[head_width : 2 * head_width],
-        early_grads[:, joint_end:].T,
+        grad_q,
+        heads[1, :head_width],
+        grad_kv[:, :head_width],
+        grad_kv[:, head_width:],
+        heads[1, 2 * head_width : 3 * head_width],
+        grad_o.T,
         featured_sums[4],
         featured_sums[2],
         featured_sums[3],
-        late_grads[:, :hidden_part],
-        headed_sums[2 * head_width :],
-        late_grads[:, hidden_part:],
+        grad_1,
+        heads[0],
+        grad_2,
         featured_sums[5],
     )
 

time: 429 us -> 308 us (0.72)
  waiting for transfers between devices: 91.9 us -> 0.04 us
  blocking collectives: 40 us -> 0 us
  Pallas kernels: 245 us -> 263 us
    reduce_scatter x2 -> x0, waiting for transfers between devices: 62.2 us -> none  [reduce_rows(): lax.psum_scatter(tensor.astype(jnp.bfloat16), 'row', scatter_dimension=0,...]
    psum x1 -> x0, blocking collectives: 40 us -> none  [local(): lax.psum(jnp.concatenate([featured, place_piece(headed, col_at, col_count...]
    psum x1 -> x0, waiting for transfers between devices: 28.5 us -> none  [all_clips(): return lax.psum(tensor.astype(jnp.bfloat16), 'dp').astype(jnp.float32)]
    pallas_call x3, Pallas kernels: 245 us -> 263 us  [call(): pl.pallas_call(kernel, in_specs=[pl.BlockSpec(memory_space=pltpu.VMEM)] *...]
    unnamed x66 -> x39, local copies, waits for them, and re-layouts: 14.9 us -> 9.91 us
  transfers between devices with their start and end apart: 7 -> 1, of which waited for: 3 -> 0; matrix products, arithmetic and copies ran while one was open for 4% -> 3% of each run, Pallas kernels for 18% -> 28%
where the time goes in v3:
time: 308 us; the launch traced here: 307 us
  Pallas kernels  263 us (85%)
  local copies, waits for them, and re-layouts  25.7 us (8%)
  between operations  14.3 us (5%)
  other arithmetic  3.71 us (1%)
    pallas_call x3, Pallas kernels, call(): pl.pallas_call(kernel, in_specs=[pl.BlockSpec(memory_space=pltpu.VMEM)] *...  263 us
    unnamed x39, local copies, waits for them, and re-layouts  9.91 us
  transfers between devices with their start and end apart: 1, of which 0 were waited for; matrix products, arithmetic and copies ran while one was open for 3% of the time, Pallas kernels for 28%

profile of v3, /device:TPU:0, one launch (start us, length us, event | category | flops | bytes accessed | tf_op | source)
XLA Modules:
  0.0 306.9 jit_solution(11548615140352980226)
XLA Ops:
  7.2 0.0 copy-start
  7.2 0.0 all-gather.2.cloned.1.call-start
  7.2 2.0 pad_maximum_fusion
  9.2 0.0 all-gather.2.cloned.1.call-update
  9.3 0.0 copy-start.1
  9.3 0.0 copy-done
  9.3 0.1 copy.38
  9.5 1.1 copy-done.1
  10.6 0.0 copy-start.9
  10.6 0.0 copy-start.10
  10.6 0.0 copy-start.11
  10.6 0.0 copy-start.12
  10.6 0.0 copy-start.13
  10.6 0.0 copy-start.14
  10.6 0.1 copy.39
  10.7 0.1 tile.21
  10.8 0.1 tile.9
  10.9 0.6 broadcast_in_dim.31.mask_ref
  11.5 0.8 dynamic_slice.21
  12.3 0.1 concatenate.13
  12.4 0.6 broadcast_in_dim.28.bkv_ref
  12.9 1.3 dynamic_slice.20
  14.3 1.6 copy.40
  15.9 0.8 dynamic_slice.22
  16.7 0.6 broadcast_in_dim.32.bh_ref
  17.2 1.7 pad_maximum_fusion.1.wkv_ref
  18.9 0.0 copy-done.9
  18.9 0.0 copy-done.10
  18.9 0.0 copy-done.11
  19.0 0.0 copy-done.12
  19.0 0.0 copy-done.13
  19.0 0.0 copy-done.14
  19.0 0.3 dynamic_update_slice.3.vec_ref
  19.3 0.0 copy-start.8
  19.3 1.0 fusion
  20.3 0.0 copy-done.8
  20.3 86.0 %front.1 = (f32[8,768]{1,0:T(8,128)}, bf16[768,192]{1,0:T(8,128)(2,1)}, bf16[768,384]{1,0:T(8,128)(2,1)}, bf16[768,192]{1,0:T(8,128)(2,1)}, bf16[768,768]{1,0:T(...) custom-call(bf16[192,768]{1,0:T(8,128)(2,1)} %get-tuple-element.119., ...), custom_call_target="tpu_custom_call" | custom-call | flops 40000000000 | bytes 60000000 | tf_op jit(solution)/shard_map/front/pallas_call | solution.py:595
  106.3 0.0 all-gather.2.cloned.1.call-done
  106.3 3.3 %fusion.2 = (bf16[768,768]{1,0:T(8,128)(2,1)}, bf16[768,768]{1,0:T(8,128)(2,1)}) fusion(bf16[768,1536]{1,0:T(8,128)(2,1)} %all-gather.2.cloned.1.call-done), kind=kLoop, calls=%fused_computation.11 | loop fusion | bytes 4718592 | tf_op jit(solution)/shard_map/slice | solution.py:718
  109.6 95.3 %middle.1 = (bf16[768,768]{1,0:T(8,128)(2,1)}, bf16[768,768]{1,0:T(8,128)(2,1)}, f32[192,768]{1,0:T(8,128)}, bf16[768,768]{1,0:T(8,128)(2,1)}, bf16[768,768]{1,0...) custom-call(bf16[192,768]{1,0:T(8,128)(2,1)} %get-tuple-element.45.normed2_ref, ...), custom_call_target="tpu_custom_call" | custom-call | flops 40000000000 | bytes 60000000 | tf_op jit(solution)/shard_map/middle/pallas_call | solution.py:595
  204.9 81.8 %back.1 = (bf16[768,768]{1,0:T(8,128)(2,1)}, bf16[768,768]{1,0:T(8,128)(2,1)}, f32[8,768]{1,0:T(8,128)}, f32[8,768]{1,0:T(8,128)}, f32[192,768]{1,0:T(8,128)}, /...) custom-call(bf16[192,768]{1,0:T(8,128)(2,1)} %get-tuple-element.119.x_ref, ...), custom_call_target="tpu_custom_call" | custom-call | flops 40000000000 | bytes 60000000 | tf_op jit(solution)/shard_map/back/pallas_call | solution.py:595
  286.7 1.3 slice_reduce_fusion
  288.1 1.3 fusion.5
  289.4 1.3 slice.63
  290.7 0.0 copy-start.2
  290.7 1.9 copy.44
  292.6 0.0 copy-done.2
  292.6 0.1 slice.64
  292.7 0.0 copy-start.5
  292.7 0.0 copy-start.7
  292.7 1.9 copy.45
  294.6 0.0 copy-start.6
  294.6 0.0 copy-start.4
  294.6 0.0 copy-done.5
  294.6 0.8 fusion.3
  295.4 0.0 copy-done.7
  295.4 0.8 copy.43
  296.2 1.6 fusion.4
  297.8 0.0 copy-done.6
  297.8 0.7 copy.50
  298.5 0.0 copy-done.4
  298.5 0.8 copy.51
  299.3 0.0 copy-done.3
  299.3 0.8 copy.52
  (9 shorter events, 0.1 us)
Async XLA Ops:
  7.2 2.1 copy-start
  7.2 99.1 %all-gather.2.cloned.1.call-start = ((), (), s32[]{:S(2)}) async-start(), calls=%async_computation | async-start | bytes 2949120 | tf_op jit(solution)/shard_map/all_gather | solution.py:23
  9.3 1.3 copy-start.1
  10.6 8.4 %copy-start.9 = (f32[192]{0:T(256)S(1)}, f32[192]{0:T(256)}, u32[]{:S(2)}) copy-start(f32[192]{0:T(256)} %param.18) | copy-start | bytes 2308
  10.6 8.4 %copy-start.10 = (f32[192]{0:T(256)S(1)}, f32[192]{0:T(256)}, u32[]{:S(2)}) copy-start(f32[192]{0:T(256)} %param.19) | copy-start | bytes 2308
  10.6 8.4 %copy-start.11 = (f32[192]{0:T(256)S(1)}, f32[192]{0:T(256)}, u32[]{:S(2)}) copy-start(f32[192]{0:T(256)} %param.27) | copy-start | bytes 2308
  10.6 8.4 %copy-start.12 = (f32[192]{0:T(256)S(1)}, f32[192]{0:T(256)}, u32[]{:S(2)}) copy-start(f32[192]{0:T(256)} %param.28) | copy-start | bytes 2308
  10.6 8.4 %copy-start.13 = (f32[192]{0:T(256)S(1)}, f32[192]{0:T(256)}, u32[]{:S(2)}) copy-start(f32[192]{0:T(256)} %param.26) | copy-start | bytes 2308
  10.6 8.4 %copy-start.14 = (f32[192]{0:T(256)S(1)}, f32[192]{0:T(256)}, u32[]{:S(2)}) copy-start(f32[192]{0:T(256)} %param.32) | copy-start | bytes 2308
  19.3 1.0 copy-start.8
  290.7 1.9 copy-start.2
  292.7 1.9 copy-start.5
  292.7 2.7 copy-start.7
  294.6 3.2 %copy-start.6 = (f32[192,192]{1,0:T(8,128)S(1)}, f32[192,192]{1,0:T(8,128)}, u32[]{:S(2)}) copy-start(f32[192,192]{1,0:T(8,128)} %get-tuple-element.142) | copy-start | bytes 442372
  294.6 3.9 %copy-start.4 = (f32[192,768]{1,0:T(8,128)S(1)}, f32[192,768]{1,0:T(8,128)}, u32[]{:S(2)}) copy-start(f32[192,768]{1,0:T(8,128)} %get-tuple-element.151) | copy-start | bytes 1769476
  295.4 3.9 %copy-start.3 = (f32[192,768]{1,0:T(8,128)S(1)}, f32[192,768]{1,0:T(8,128)}, u32[]{:S(2)}) copy-start(f32[192,768]{1,0:T(8,128)} %get-tuple-element.153) | copy-start | bytes 1769476
Sparse Core Ops, SparseCore 0:
  10.2 33.6 all-gather.1
